TPU v7x, 128 devices: a whole 4x4x4 slice. The times are simulated.
128 devices in a mesh: dp: 16 (over z, y_hi, core), tensor: 8 (over x, y_lo).
Axes of the slice: x: 4, y: 4 (y_hi: 2, y_lo: 2; y = y_hi * 2 + y_lo), z: 4, core: 2. Of those that a mesh axis runs over, the one named last changes fastest.
Arguments:
- prefix_in: bfloat16 [8192, 4608], P(('dp', 'tensor')), may hold values from -24 to 24
- action_in: bfloat16 [768, 2048], P('dp'), may hold values from -6 to 6
- segment_ids: int32 [16, 512], P('dp'), may hold values from 0 to 7, never falling along the last dimension, each value on 1 to 128 neighbouring positions
- gain_prefix: float32 [4608], replicated, may hold values from 0.5 to 1.5
- gain_action: float32 [2048], replicated, may hold values from 0.5 to 1.5
- query_prefix: bfloat16 [4608, 4096], P(None, 'tensor'), may hold values from -0.7365696 to 0.7365696
- key_prefix: bfloat16 [4608, 2048], P(None, 'tensor'), may hold values from -0.19150809 to 0.19150809
- value_prefix: bfloat16 [4608, 2048], P(None, 'tensor'), may hold values from -0.09375 to 0.09375
- out_prefix: bfloat16 [4608, 4096], P(None, 'tensor'), may hold values from -0.09375 to 0.09375
- query_action: bfloat16 [2048, 4096], P(None, 'tensor'), may hold values from -1.1048543 to 1.1048543
- key_action: bfloat16 [2048, 2048], P(None, 'tensor'), may hold values from -0.28726213 to 0.28726213
- value_action: bfloat16 [2048, 2048], P(None, 'tensor'), may hold values from -0.125 to 0.125
- out_action: bfloat16 [2048, 4096], P(None, 'tensor'), may hold values from -0.125 to 0.125
- cot_prefix: bfloat16 [8192, 4608], P(('dp', 'tensor')), may hold values from -6 to 6
- cot_action: bfloat16 [768, 2048], P('dp'), may hold values from -6 to 6
Outputs:
- prefix_grad: bfloat16 [8192, 4608], P(('dp', 'tensor'))
- action_grad: bfloat16 [768, 2048], P('dp')
- query_prefix_grad: bfloat16 [4608, 4096], P('dp', 'tensor')
- key_prefix_grad: bfloat16 [4608, 2048], P('dp', 'tensor')
- value_prefix_grad: bfloat16 [4608, 2048], P('dp', 'tensor')
- out_prefix_grad: bfloat16 [4608, 4096], P('dp', 'tensor')
- query_action_grad: bfloat16 [2048, 4096], P('dp', 'tensor')
- key_action_grad: bfloat16 [2048, 2048], P('dp', 'tensor')
- value_action_grad: bfloat16 [2048, 2048], P('dp', 'tensor')
- out_action_grad: bfloat16 [2048, 4096], P('dp', 'tensor')
Inputs may be any that keep to these rules, and one draw needn't show every extreme that they name: `segment_ids`: along each sample's positions the ids never fall.
All inputs are finite; a program needn't handle non-finite values.
Results may differ from a plain program's by a relative error of at most 0.02.
The roundings to bfloat16 on the way count: a program that leaves them out, or rounds other values in their place, can miss the bound.
Values may be sent and summed in bfloat16 or wider, within the bound.
A program may use at most 192 MiB of HBM per device.

v0:
```python
import math

import jax
import jax.numpy as jnp
from jax import lax
from jax.sharding import PartitionSpec as P

D = 4608
H = 32
HD = 128


EPSILON = 1e-06
SOFT_CAP = 50.0


def for_sending(array):

    def short(part):
        return part.astype(jnp.bfloat16) if part.dtype == jnp.float32 else part

    return jax.tree.map(short, array)


def norm_rows(inputs, gain):
    widened = inputs.astype(jnp.float32)
    inverse = lax.rsqrt(jnp.mean(widened * widened, -1, keepdims=True) + EPSILON)
    return (widened, inverse, (widened * inverse * gain).astype(jnp.bfloat16))


def norm_back(widened, inverse, gain, upstream):
    normed = widened * inverse
    scaled = upstream * gain
    return (inverse * (scaled - normed * jnp.mean(scaled * normed, -1, keepdims=True))).astype(
        jnp.bfloat16
    )


def project(inputs, weight):
    return jnp.dot(inputs, weight, preferred_element_type=jnp.float32).astype(jnp.bfloat16)


def by_heads(matrix):
    return matrix.reshape(matrix.shape[0], matrix.shape[1] // HD, HD)


def outer_sum(left_rows, right_rows):
    return lax.dot_general(
        left_rows, right_rows, (((0,), (0,)), ((), ())), preferred_element_type=jnp.float32
    )


def back_project(grad_rows, weight):
    return lax.dot_general(
        grad_rows, weight, (((1,), (1,)), ((), ())), preferred_element_type=jnp.float32
    )


def attend(queries, all_keys, all_values, grad_out, allowed):
    q_count, q_heads, head_width = queries.shape
    kv_heads = all_keys.shape[1]
    group_size = q_heads // kv_heads
    score_scale = 1.0 / math.sqrt(D // H)
    q_group = queries.reshape(q_count, kv_heads, group_size, head_width)
    raw_scores = (
        jnp.einsum("qkgd,jkd->kgqj", q_group, all_keys, preferred_element_type=jnp.float32)
        * score_scale
    )
    capped = SOFT_CAP * jnp.tanh(raw_scores / SOFT_CAP)
    weights = jnp.exp(capped)
    if allowed is not None:
        weights = jnp.where(allowed, weights, 0.0)
    probs = weights / jnp.sum(weights, -1, keepdims=True)
    prob_half = probs.astype(jnp.bfloat16)
    attended = jnp.einsum(
        "kgqj,jkd->qkgd", prob_half, all_values, preferred_element_type=jnp.float32
    )
    attended = attended.astype(jnp.bfloat16).reshape(q_count, q_heads * head_width)
    out_group = grad_out.reshape(q_count, kv_heads, group_size, head_width)
    grad_probs = jnp.einsum(
        "qkgd,jkd->kgqj", out_group, all_values, preferred_element_type=jnp.float32
    )
    inner = jnp.sum(probs * grad_probs, -1, keepdims=True)
    slope = 1.0 - capped / SOFT_CAP * (capped / SOFT_CAP)
    grad_raw = (probs * (grad_probs - inner) * slope * score_scale).astype(jnp.bfloat16)
    grad_queries = jnp.einsum(
        "kgqj,jkd->qkgd", grad_raw, all_keys, preferred_element_type=jnp.float32
    )
    grad_queries = grad_queries.astype(jnp.bfloat16).reshape(q_count, q_heads * head_width)
    grad_keys = jnp.einsum("kgqj,qkgd->jkd", grad_raw, q_group, preferred_element_type=jnp.float32)
    grad_values = jnp.einsum(
        "kgqj,qkgd->jkd", prob_half, out_group, preferred_element_type=jnp.float32
    )
    return (attended, grad_queries, grad_keys, grad_values)


def per_device(
    prefix_in,
    action_in,
    segment_ids,
    gain_prefix,
    gain_action,
    query_prefix,
    key_prefix,
    value_prefix,
    out_prefix,
    query_action,
    key_action,
    value_action,
    out_action,
    cot_prefix,
    cot_action,
):
    pre_wide, pre_inv, pre_normed = norm_rows(prefix_in, gain_prefix)
    act_wide, act_inv, act_normed = norm_rows(action_in, gain_action)
    pre_rows, cot_rows = (
        lax.all_gather(pre_normed, "tensor", axis=0, tiled=True),
        lax.all_gather(cot_prefix, "tensor", axis=0, tiled=True),
    )
    pre_query = project(pre_rows, query_prefix)
    pre_key = project(pre_rows, key_prefix)
    pre_value = project(pre_rows, value_prefix)
    pre_dout = project(cot_rows, out_prefix)
    act_query = project(act_normed, query_action)
    act_key = project(act_normed, key_action)
    act_value = project(act_normed, value_action)
    act_dout = project(cot_action, out_action)
    seg_row = segment_ids[0]
    allowed = seg_row[None, :] <= seg_row[:, None]
    pre_attn, pre_dquery, pre_dkey, pre_dvalue = attend(
        by_heads(pre_query), by_heads(pre_key), by_heads(pre_value), by_heads(pre_dout), allowed
    )
    joint_keys = jnp.concatenate([by_heads(pre_key), by_heads(act_key)], 0)
    joint_values = jnp.concatenate([by_heads(pre_value), by_heads(act_value)], 0)
    act_attn, act_dquery, joint_dkey, joint_dvalue = attend(
        by_heads(act_query), joint_keys, joint_values, by_heads(act_dout), None
    )
    seq_len = pre_rows.shape[0]
    act_len = action_in.shape[0]
    pre_dkey = (pre_dkey + joint_dkey[:seq_len]).astype(jnp.bfloat16).reshape(seq_len, -1)
    pre_dvalue = (pre_dvalue + joint_dvalue[:seq_len]).astype(jnp.bfloat16).reshape(seq_len, -1)
    act_dkey = joint_dkey[seq_len:].astype(jnp.bfloat16).reshape(act_len, -1)
    act_dvalue = joint_dvalue[seq_len:].astype(jnp.bfloat16).reshape(act_len, -1)
    terms = (
        outer_sum(pre_rows, pre_dquery),
        outer_sum(pre_rows, pre_dkey),
        outer_sum(pre_rows, pre_dvalue),
        outer_sum(cot_rows, pre_attn),
        outer_sum(act_normed, act_dquery),
        outer_sum(act_normed, act_dkey),
        outer_sum(act_normed, act_dvalue),
        outer_sum(cot_action, act_attn),
    )
    rounded = tuple((total.astype(jnp.bfloat16) for total in terms))
    summed = jax.tree.map(
        lambda part: part.astype(jnp.float32),
        lax.psum_scatter(for_sending(rounded), "dp", scatter_dimension=0, tiled=True),
    )
    grads = tuple((total.astype(jnp.bfloat16) for total in summed))
    pre_up = (
        back_project(pre_dquery, query_prefix)
        + back_project(pre_dkey, key_prefix)
        + back_project(pre_dvalue, value_prefix)
    )
    act_up = (
        back_project(act_dquery, query_action)
        + back_project(act_dkey, key_action)
        + back_project(act_dvalue, value_action)
    )
    own_up = lax.psum_scatter(
        pre_up.astype(jnp.bfloat16), "tensor", scatter_dimension=0, tiled=True
    ).astype(jnp.float32)
    act_total = lax.psum(act_up.astype(jnp.bfloat16), "tensor").astype(jnp.float32)
    action_grad = norm_back(act_wide, act_inv, gain_action, act_total)
    prefix_grad = norm_back(pre_wide, pre_inv, gain_prefix, own_up)
    return (
        prefix_grad,
        action_grad,
        grads[0],
        grads[1],
        grads[2],
        grads[3],
        grads[4],
        grads[5],
        grads[6],
        grads[7],
    )


def solution(mesh):
    in_specs = (
        P(("dp", "tensor"), None),
        P("dp", None),
        P("dp", None),
        P(),
        P(),
        P(None, "tensor"),
        P(None, "tensor"),
        P(None, "tensor"),
        P(None, "tensor"),
        P(None, "tensor"),
        P(None, "tensor"),
        P(None, "tensor"),
        P(None, "tensor"),
        P(("dp", "tensor"), None),
        P("dp", None),
    )
    out_specs = (
        P(("dp", "tensor"), None),
        P("dp", None),
        P("dp", "tensor"),
        P("dp", "tensor"),
        P("dp", "tensor"),
        P("dp", "tensor"),
        P("dp", "tensor"),
        P("dp", "tensor"),
        P("dp", "tensor"),
        P("dp", "tensor"),
    )
    return jax.shard_map(
        per_device, mesh=mesh, in_specs=in_specs, out_specs=out_specs, check_vma=False
    )
```

profile of v0, /device:TPU:1, one launch (start us, length us, event | category | flops | bytes accessed | tf_op | source)
XLA Modules:
  0.0 1064.9 jit_solution(17318298808570454314)
XLA Ops:
  8.7 2.1 fusion.29
  12.7 1.7 fusion.37
  14.5 1.6 fusion.38
  16.0 2.1 convolution_convert_fusion.16
  18.2 2.1 convolution_convert_fusion.15
  21.2 92.5 %all-gather.3.cloned.1.call-done = bf16[512,4608]{1,0:T(8,128)(2,1)} async-done(((bf16[64,4608]{1,0:T(8,128)(2,1)}), bf16[512,4608]{1,0:T(8,128)(2,1)}) %all-gather.3.cloned.1.call-update) | async-done | bytes 4718608 | tf_op jit(solution)/shard_map/all_gather | solution.py:117
  113.7 4.5 convolution_convert_fusion.11
  118.4 4.5 convolution_convert_fusion.12
  122.9 1.8 copy.73
  125.7 2.1 bitcast_reduce_fusion
  127.8 3.1 convolution_bitcast_fusion.1
  134.0 2.2 fusion.35
  136.2 79.7 %all-gather.5.cloned.1.call-done = bf16[512,4608]{1,0:T(8,128)(2,1)} async-done(((bf16[64,4608]{1,0:T(8,128)(2,1)}), bf16[512,4608]{1,0:T(8,128)(2,1)}) %all-gather.5.cloned.1.call-update) | async-done | bytes 4718608 | tf_op jit(solution)/shard_map/all_gather | solution.py:118
  215.9 6.4 convolution_convert_fusion.8
  222.3 2.8 fusion.96
  225.1 6.5 convolution_convert_fusion.9
  231.6 2.0 fusion.7
  233.7 2.0 copy-done.21
  235.7 2.2 fusion.27
  237.9 11.3 %fusion.26 = bf16[512,2,128]{0,2,1:T(8,128)(2,1)} fusion(bf16[512,2,2,128]{0,3,2,1:T(8,128)(2,1)} %bitcast.275, f32[2,512,512,2]{2,1,3,0:T(8,128)} %fusion.96, f32[2,512,512,2]{2,1,3,0:T(8,128)} %copy-done.21, f32[560,2,128]{0,2,1:T(8,128)} %convolution_bitcast_fusion.1, f32[2,2,512]{2,1,0:T(2,128)S(1)} %get-tuple-element.40, ...), kind=kOutput, calls=%fused_computation.51 | convolution fusion | flops 285477376 | bytes 18628608 | tf_op jit(solution)/shard_map/kgqj,qkgd->jkd/dot_general | solution.py:90
  249.2 9.2 fusion.17
  258.5 1.6 fusion.100
  260.1 1.6 fusion.99
  261.8 3.0 fusion.10
  265.0 4.7 fusion.97
  269.8 5.1 fusion.98
  274.9 7.7 add_convert_fusion
  284.3 1.5 convolution_convert_fusion.6
  285.9 2.2 convolution_convert_fusion.5
  289.3 2.6 copy.113
  291.9 5.3 convolution_convert_fusion.2
  297.3 5.3 convolution_convert_fusion.3
  302.9 3.7 convolution_convert_fusion.10
  306.6 6.6 fusion.2
  313.2 6.7 copy.111
  320.9 6.7 convolution_convert_fusion.1
  327.7 6.4 all-reduce.2.cloned.1.call-done
  335.2 1.7 fusion.54
  337.0 104.2 %reduce-scatter.14.cloned.1.call-done = bf16[64,4608]{1,0:T(8,128)(2,1)} async-done(((bf16[512,4608]{1,0:T(8,128)(2,1)}), bf16[64,4608]{1,0:T(8,128)(2,1)}) %reduce-scatter.14.cloned.1.call-update) | async-done | bytes 589840 | tf_op jit(solution)/shard_map/reduce_scatter | solution.py:170
  442.6 2.2 fusion.33
  444.8 67.2 %reduce-scatter.24.cloned.1.call-done = bf16[128,256]{1,0:T(8,128)(2,1)} async-done(((bf16[2048,256]{1,0:T(8,128)(2,1)}), bf16[128,256]{1,0:T(8,128)(2,1)}) %reduce-scatter.24.cloned.1.call-update) | async-done | bytes 65552 | tf_op jit(solution)/shard_map/reduce_scatter | solution.py:157
  511.9 70.3 %reduce-scatter.26.cloned.1.call-done = bf16[128,256]{1,0:T(8,128)(2,1)} async-done(((bf16[2048,256]{1,0:T(8,128)(2,1)}), bf16[128,256]{1,0:T(8,128)(2,1)}) %reduce-scatter.26.cloned.1.call-update) | async-done | bytes 65552 | tf_op jit(solution)/shard_map/reduce_scatter | solution.py:157
  582.2 75.0 %reduce-scatter.22.cloned.1.call-done = bf16[128,512]{1,0:T(8,128)(2,1)} async-done(((bf16[2048,512]{1,0:T(8,128)(2,1)}), bf16[128,512]{1,0:T(8,128)(2,1)}) %reduce-scatter.22.cloned.1.call-update) | async-done | bytes 131088 | tf_op jit(solution)/shard_map/reduce_scatter | solution.py:157
  657.2 74.6 %reduce-scatter.30.cloned.1.call-done = bf16[128,512]{1,0:T(8,128)(2,1)} async-done(((bf16[2048,512]{1,0:T(8,128)(2,1)}), bf16[128,512]{1,0:T(8,128)(2,1)}) %reduce-scatter.30.cloned.1.call-update) | async-done | bytes 131088
  731.8 76.4 %reduce-scatter.20.cloned.1.call-done = bf16[288,256]{1,0:T(8,128)(2,1)} async-done(((bf16[4608,256]{1,0:T(8,128)(2,1)}), bf16[288,256]{1,0:T(8,128)(2,1)}) %reduce-scatter.20.cloned.1.call-update) | async-done | bytes 147472 | tf_op jit(solution)/shard_map/reduce_scatter | solution.py:157
  808.3 75.8 %reduce-scatter.18.cloned.1.call-done = bf16[288,256]{1,0:T(8,128)(2,1)} async-done(((bf16[4608,256]{1,0:T(8,128)(2,1)}), bf16[288,256]{1,0:T(8,128)(2,1)}) %reduce-scatter.18.cloned.1.call-update) | async-done | bytes 147472 | tf_op jit(solution)/shard_map/reduce_scatter | solution.py:157
  884.0 87.7 %reduce-scatter.28.cloned.1.call-done = bf16[288,512]{1,0:T(8,128)(2,1)} async-done(((bf16[4608,512]{1,0:T(8,128)(2,1)}), bf16[288,512]{1,0:T(8,128)(2,1)}) %reduce-scatter.28.cloned.1.call-update) | async-done | bytes 294928
  971.7 86.1 %reduce-scatter.16.cloned.1.call-done = bf16[288,512]{1,0:T(8,128)(2,1)} async-done(((bf16[4608,512]{1,0:T(8,128)(2,1)}), bf16[288,512]{1,0:T(8,128)(2,1)}) %reduce-scatter.16.cloned.1.call-update) | async-done | bytes 294928 | tf_op jit(solution)/shard_map/reduce_scatter | solution.py:157
  (96 shorter events, 15.9 us)
Async XLA Ops:
  7.2 111.2 %copy-start = (bf16[4608,256]{1,0:T(8,128)(2,1)S(1)}, bf16[4608,256]{1,0:T(8,128)(2,1)}, u32[]{:S(2)}) copy-start(bf16[4608,256]{1,0:T(8,128)(2,1)} %param.21) | copy-start | bytes 7077892
  7.2 7.3 copy-start.2
  7.2 7.3 copy-start.6
  7.2 11.0 %copy-start.5 = (bf16[48,2048]{1,0:T(8,128)(2,1)S(1)}, bf16[48,2048]{1,0:T(8,128)(2,1)}, u32[]{:S(2)}) copy-start(bf16[48,2048]{1,0:T(8,128)(2,1)} %param.29) | copy-start | bytes 589828
  7.2 106.5 %all-gather.3.cloned.1.call-start = ((), (), s32[]{:S(2)}) async-start(), calls=%async_computation.9 | async-start | bytes 5308416 | tf_op jit(solution)/shard_map/all_gather | solution.py:117
  10.8 9.4 copy-start.16
  10.8 205.1 %all-gather.5.cloned.1.call-start = ((), (), s32[]{:S(2)}) async-start(), calls=%async_computation.10 | async-start | bytes 5308416 | tf_op jit(solution)/shard_map/all_gather | solution.py:118
  11.6 322.5 %all-reduce.2.cloned.1.call-start = ((), (), s32[]{:S(2)}) async-start(), calls=%async_computation.12 | async-start | bytes 393216 | tf_op jit(solution)/shard_map/psum | solution.py:173
  133.2 0.8 copy-start.17
  225.1 6.5 copy-start.12
  225.1 6.5 copy-start.14
  231.6 2.1 copy-start.19
  231.6 4.1 copy-start.18
  233.6 2.1 copy-start.21
  233.6 15.6 %copy-start.22 = (f32[2,2,512]{2,1,0:T(2,128)}, f32[2,2,512]{2,1,0:T(2,128)S(1)}, u32[]{:S(2)}) copy-start(f32[2,2,512]{2,1,0:T(2,128)S(1)} %get-tuple-element.40) | copy-start | bytes 24580
  264.8 176.3 %reduce-scatter.14.cloned.1.call-start = ((), (), s32[]{:S(2)}) async-start(), calls=%async_computation.11 | async-start | bytes 5308416 | tf_op jit(solution)/shard_map/reduce_scatter | solution.py:170
  265.0 4.7 copy-start.10
  269.8 5.1 copy-start.4
  269.8 5.1 copy-start.8
  282.6 229.3 %reduce-scatter.24.cloned.1.call-start = ((), (), s32[]{:S(2)}) async-start(), calls=%async_computation.17 | async-start | bytes 1114112 | tf_op jit(solution)/shard_map/reduce_scatter | solution.py:157
  284.2 3.9 copy-start.20
  284.2 298.0 %reduce-scatter.26.cloned.1.call-start = ((), (), s32[]{:S(2)}) async-start(), calls=%async_computation.18 | async-start | bytes 1114112 | tf_op jit(solution)/shard_map/reduce_scatter | solution.py:157
  285.8 371.3 %reduce-scatter.22.cloned.1.call-start = ((), (), s32[]{:S(2)}) async-start(), calls=%async_computation.16 | async-start | bytes 2228224 | tf_op jit(solution)/shard_map/reduce_scatter | solution.py:157
  288.1 443.7 %reduce-scatter.30.cloned.1.call-start = ((), (), s32[]{:S(2)}) async-start(), calls=%async_computation.20 | async-start | bytes 2228224
  288.5 3.4 copy-start.9
  291.9 5.4 copy-start.11
  291.9 516.4 %reduce-scatter.20.cloned.1.call-start = ((), (), s32[]{:S(2)}) async-start(), calls=%async_computation.15 | async-start | bytes 2506752 | tf_op jit(solution)/shard_map/reduce_scatter | solution.py:157
  297.2 5.6 copy-start.13
  297.2 5.6 copy-start.23
  297.2 586.8 %reduce-scatter.18.cloned.1.call-start = ((), (), s32[]{:S(2)}) async-start(), calls=%async_computation.14 | async-start | bytes 2506752 | tf_op jit(solution)/shard_map/reduce_scatter | solution.py:157
  302.6 669.1 %reduce-scatter.28.cloned.1.call-start = ((), (), s32[]{:S(2)}) async-start(), calls=%async_computation.19 | async-start | bytes 5013504
  319.9 1.0 copy-start.7
  319.9 737.9 %reduce-scatter.16.cloned.1.call-start = ((), (), s32[]{:S(2)}) async-start(), calls=%async_computation.13 | async-start | bytes 5013504 | tf_op jit(solution)/shard_map/reduce_scatter | solution.py:157
  327.6 113.5 %copy-start.3 = (bf16[64,4608]{1,0:T(8,128)(2,1)S(1)}, bf16[64,4608]{1,0:T(8,128)(2,1)}, u32[]{:S(2)}) copy-start(bf16[64,4608]{1,0:T(8,128)(2,1)} %param.15) | copy-start | bytes 1769476
  327.7 113.5 %copy-start.15 = (f32[4608]{0:T(1024)S(1)}, f32[4608]{0:T(1024)}, u32[]{:S(2)}) copy-start(f32[4608]{0:T(1024)} %param.18) | copy-start | bytes 55300
  327.7 730.2 %copy-start.1 = (bf16[4608,256]{1,0:T(8,128)(2,1)S(1)}, bf16[4608,256]{1,0:T(8,128)(2,1)}, u32[]{:S(2)}) copy-start(bf16[4608,256]{1,0:T(8,128)(2,1)} %param.21) | copy-start | bytes 7077892
Sparse Core Ops, SparseCore 0:
  11.0 102.7 all-gather.2
  115.4 100.4 all-gather.4
  264.9 69.1 all-reduce.1
  336.5 104.6 reduce-scatter.13
  445.8 66.0 reduce-scatter.23
  516.1 66.0 reduce-scatter.25
  587.2 69.9 reduce-scatter.21
  661.6 70.1 reduce-scatter.29
  736.9 71.2 reduce-scatter.19
  812.7 71.2 reduce-scatter.17
  889.3 82.3 reduce-scatter.27
  976.2 81.5 reduce-scatter.15
where the time goes:
time: 1080 us; the launch traced here: 1060 us
  waiting for transfers between devices  897 us (83%)
  matrix products  124 us (11%)
  local copies, waits for them, and re-layouts  16.3 us (2%)
  between operations  14.9 us (1%)
  other arithmetic  12.1 us (1%)
    reduce_scatter x6, waiting for transfers between devices, per_device(): lax.psum_scatter(for_sending(rounded), 'dp', scatter_dimension=0, tiled=T...  451 us
    unnamed x14, waiting for transfers between devices  163 us
    reduce_scatter x1, waiting for transfers between devices, per_device(): lax.psum_scatter(pre_up.astype(jnp.bfloat16), 'tensor', scatter_dimension...  104 us
    all_gather x1, waiting for transfers between devices, per_device(): lax.all_gather(pre_normed, 'tensor', axis=0, tiled=True)  92.5 us
    all_gather x1, waiting for transfers between devices, per_device(): lax.all_gather(cot_prefix, 'tensor', axis=0, tiled=True)  79.7 us
    dot_general x8, matrix products, outer_sum(): lax.dot_general(left_rows, right_rows, (((0,), (0,)), ((), ())), preferre...  29.8 us
    dot_general x8, matrix products, project(): jnp.dot(inputs, weight, preferred_element_type=jnp.float32)  29.3 us
    dot_general x6, matrix products, back_project(): lax.dot_general(grad_rows, weight, (((1,), (1,)), ((), ())), preferred_el...  23.8 us
  transfers between devices with their start and end apart: 12, of which 12 were waited for; matrix products, arithmetic and copies ran while one was open for 9% of the time, Pallas kernels for 0%

commit v1 on v0

v1 whole, which is shorter than its diff:
```python
import functools
import math

import jax
import jax.numpy as jnp
from jax import lax
from jax.experimental import pallas as pl
from jax.experimental.pallas import tpu as pltpu
from jax.sharding import PartitionSpec as P

D = 4608
DA = 2048
H = 32
HD = 128
ROWS = 64
ACT = 48
SLOTS = 8
PREF = SLOTS * ROWS
QW, KW = 512, 256
COLS = 2 * QW + 2 * KW
HALF = COLS // 2
TILE = 256
EPSILON = 1e-06
SOFT_CAP = 50.0
SCALE = 1.0 / math.sqrt(D // H)
MESH = pl.DeviceIdType.MESH
BF16, F32 = jnp.bfloat16, jnp.float32
VMEM = pl.BlockSpec(memory_space=pltpu.VMEM)
ANY = pl.BlockSpec(memory_space=pl.ANY)


def x_step(k):
    return lax.axis_index("dp"), lax.rem(lax.axis_index("tensor") + 2 * k + 8, 8)


def z_step(k):
    return lax.rem(lax.axis_index("dp") + 4 * k + 16, 16), lax.axis_index("tensor")


def y_low():
    t = lax.axis_index("tensor")
    return lax.axis_index("dp"), t + 1 - 2 * lax.rem(t, 2)


def y_high():
    d = lax.axis_index("dp")
    return d + 2 - 4 * lax.rem(lax.div(d, 2), 2), lax.axis_index("tensor")


def sibling():
    d = lax.axis_index("dp")
    return d + 1 - 2 * lax.rem(d, 2), lax.axis_index("tensor")


def slot_order():
    t = lax.axis_index("tensor")
    x, y = lax.div(t, 2), lax.rem(t, 2)

    def at(step, row):
        return 2 * lax.rem(x + step + 4, 4) + row

    return jnp.stack(
        [at(0, y), at(0, 1 - y), at(-1, y), at(1, y), at(2, y), at(-1, 1 - y), at(1, 1 - y), at(2, 1 - y)]
    )


def greet(partners):
    barrier = pltpu.get_barrier_semaphore()
    for device in partners:
        pl.semaphore_signal(barrier, inc=1, device_id=device, device_id_type=MESH)
    pl.semaphore_wait(barrier, len(partners))


def remote(src, dst, send, recv, device):
    return pltpu.make_async_remote_copy(
        src_ref=src, dst_ref=dst, send_sem=send, recv_sem=recv, device_id=device, device_id_type=MESH
    )


def norm(rows, gain):
    widened = rows.astype(F32)
    inverse = lax.rsqrt(jnp.mean(widened * widened, -1, keepdims=True) + EPSILON)
    return (widened * inverse * gain).astype(BF16)


def gather_kernel(
    pin, cot, gain, ain, acot, again, wq, wk, wv, wo, aq, ak, av, ao,
    proj, aproj, g_norm, g_cot, s_norm, s_cot, a_norm, sa_norm, sa_cot,
    norm_v, cot_v, w_v, aw_v, send, recv, sib_send, sib_recv, local, w_sem, act_send, act_recv,
):
    weights = []
    for i, (ref, first) in enumerate(((aq, 0), (ak, QW), (av, QW + KW), (ao, QW + 2 * KW))):
        weights.append(pltpu.make_async_copy(ref, aw_v.at[:, pl.ds(first, ref.shape[1])], w_sem.at[i]))
    for i, (ref, first) in enumerate(((wq, 0), (wk, QW), (wv, QW + KW), (wo, QW + 2 * KW))):
        weights.append(pltpu.make_async_copy(ref, w_v.at[:, pl.ds(first, ref.shape[1])], w_sem.at[4 + i]))
    for copy in weights:
        copy.start()
    left, right, across, twin = x_step(-1), x_step(1), y_low(), sibling()
    greet((left, right, across, twin))

    arrays = ((norm_v, g_norm, s_norm), (cot_v, g_cot, s_cot))

    def hop(a, src, dst, device):
        held = arrays[a][0]
        return remote(held.at[src], held.at[dst], send.at[a, dst], recv.at[a, dst], device)

    hops = [
        {1: hop(a, 0, 1, across), 2: hop(a, 0, 2, right), 3: hop(a, 0, 3, left),
         4: hop(a, 2, 4, right) if a == 0 else hop(a, 3, 4, left),
         5: hop(a, 1, 5, right), 6: hop(a, 1, 6, left), 7: hop(a, 4, 7, across)}
        for a in range(2)
    ]
    twins = [
        [remote(held.at[s], far.at[s], sib_send.at[a, s], sib_recv.at[a, s], twin) for s in range(SLOTS)]
        for a, (held, _, far) in enumerate(arrays)
    ]
    stores = [
        [pltpu.make_async_copy(held.at[s], near.at[s], local.at[a, s]) for s in range(SLOTS)]
        for a, (held, near, _) in enumerate(arrays)
    ]

    def spread(a, s):
        twins[a][s].start()
        stores[a][s].start()

    cot_v[0] = cot[...]
    for s in (1, 2, 3):
        hops[1][s].start()
    norm_v[0] = norm(pin[...], gain[...])
    for s in (1, 2, 3):
        hops[0][s].start()
    spread(1, 0)
    spread(0, 0)

    a_norm[...] = norm(ain[...], again[...])
    act_twins = [
        remote(a_norm, sa_norm, act_send.at[0], act_recv.at[0], twin),
        remote(acot, sa_cot, act_send.at[1], act_recv.at[1], twin),
    ]
    for copy in act_twins:
        copy.start()
    for copy in weights[:4]:
        copy.wait()

    def act_project(rows, first):
        def step(j, carry):
            cols = pl.ds(pl.multiple_of(j * TILE, TILE), TILE)
            aproj[:, cols] = jnp.dot(rows[...], aw_v[:, cols], preferred_element_type=F32).astype(BF16)
            return carry

        lax.fori_loop(first, first + (4 if first == 0 else 2), step, 0)

    act_project(a_norm, 0)
    act_project(acot, 4)

    def project(held, low, high, first):
        def step(j, carry):
            cols = pl.ds(pl.multiple_of(j * TILE, TILE), TILE)
            rows = held[low:high].reshape((high - low) * ROWS, D)
            out = jnp.dot(rows, w_v[:, cols], preferred_element_type=F32).astype(BF16)
            proj[low:high, :, cols] = out.reshape(high - low, ROWS, TILE)
            return carry

        lax.fori_loop(first, first + (4 if first == 0 else 2), step, 0)

    hops[1][3].wait_recv()
    hops[1][4].start()
    hops[0][2].wait_recv()
    hops[0][4].start()
    for a in (1, 0):
        hops[a][1].wait_recv()
        hops[a][5].start()
        hops[a][6].start()
    hops[1][2].wait_recv()
    hops[0][3].wait_recv()
    for a in (1, 0):
        for s in (1, 2, 3):
            spread(a, s)
    for copy in weights[4:]:
        copy.wait()
    project(cot_v, 0, 4, 4)
    for a in (1, 0):
        hops[a][4].wait_recv()
        hops[a][7].start()
        spread(a, 4)
    project(norm_v, 0, 4, 0)
    for a, first in ((1, 4), (0, 0)):
        for s in (5, 6, 7):
            hops[a][s].wait_recv()
            spread(a, s)
        project(arrays[a][0], 4, 8, first)
    for a in range(2):
        for s in range(1, SLOTS):
            hops[a][s].wait_send()
        for s in range(SLOTS):
            twins[a][s].wait()
            stores[a][s].wait()
    for copy in act_twins:
        copy.wait()


def gather_and_project(pin, cot, gain, ain, acot, again, *weights):
    rows = jax.ShapeDtypeStruct((SLOTS, ROWS, D), BF16)
    acts = jax.ShapeDtypeStruct((ACT, DA), BF16)
    dma = pltpu.SemaphoreType.DMA
    return pl.pallas_call(
        gather_kernel,
        out_shape=(
            jax.ShapeDtypeStruct((SLOTS, ROWS, COLS), BF16), jax.ShapeDtypeStruct((ACT, COLS), BF16),
            rows, rows, rows, rows, acts, acts, acts,
        ),
        in_specs=[VMEM] * 6 + [ANY] * 8,
        out_specs=(VMEM, VMEM, ANY, ANY, ANY, ANY, VMEM, ANY, ANY),
        scratch_shapes=[
            pltpu.VMEM((SLOTS, ROWS, D), BF16), pltpu.VMEM((SLOTS, ROWS, D), BF16),
            pltpu.VMEM((D, COLS), BF16), pltpu.VMEM((DA, COLS), BF16),
            dma((2, SLOTS)), dma((2, SLOTS)), dma((2, SLOTS)), dma((2, SLOTS)), dma((2, SLOTS)),
            dma((8,)), dma((2,)), dma((2,)),
        ],
        compiler_params=pltpu.CompilerParams(
            collective_id=0, has_side_effects=True, vmem_limit_bytes=56 << 20
        ),
        name="gather_and_project",
    )(pin, cot, gain[None, :], ain, acot, again[None, :], *weights)


def dot_last(a, b):
    return lax.dot_general(a, b, (((1,), (1,)), ((), ())), preferred_element_type=F32)


def soft(key_rows, query_rows):
    t = jnp.tanh(dot_last(key_rows, query_rows) * (SCALE / SOFT_CAP))
    return t, jnp.exp(SOFT_CAP * t)


def attend_kernel(proj, aproj, seg_row, seg_col, grads, agrads, dk, dv):
    block = 256
    for h in range(2):
        key = proj[:, QW + HD * h : QW + HD * (h + 1)]
        value = proj[:, QW + KW + HD * h : QW + KW + HD * (h + 1)]
        key_t, value_t = key.T, value.T
        base = HALF * h
        akey = aproj[:, QW + HD * h : QW + HD * (h + 1)]
        avalue = aproj[:, QW + KW + HD * h : QW + KW + HD * (h + 1)]

        def two(first):
            return jnp.concatenate([aproj[:, first + HD * (2 * h + g) : first + HD * (2 * h + g + 1)] for g in range(2)], 0)

        aq, ado = two(0), two(QW + 2 * KW)
        tp, wp = soft(key, aq)
        ta, wa = soft(akey, aq)
        rate = 1.0 / (jnp.sum(wp, 0, keepdims=True) + jnp.sum(wa, 0, keepdims=True))
        pp, pa = wp * rate, wa * rate
        gp, ga = dot_last(value, ado), dot_last(avalue, ado)
        inner = jnp.sum(pp * gp, 0, keepdims=True) + jnp.sum(pa * ga, 0, keepdims=True)
        sp = (pp * (gp - inner) * (1.0 - tp * tp) * SCALE).astype(BF16)
        sa = (pa * (ga - inner) * (1.0 - ta * ta) * SCALE).astype(BF16)
        pp, pa = pp.astype(BF16), pa.astype(BF16)
        dk[...] = jnp.dot(sp, aq, preferred_element_type=F32)
        dv[...] = jnp.dot(pp, ado, preferred_element_type=F32)
        agrads[:, base + 256 : base + 384] = jnp.dot(sa, aq, preferred_element_type=F32).astype(BF16)
        agrads[:, base + 384 : base + 512] = jnp.dot(pa, ado, preferred_element_type=F32).astype(BF16)
        adq = (jnp.dot(key_t, sp, preferred_element_type=F32) + jnp.dot(akey.T, sa, preferred_element_type=F32)).T
        aat = (jnp.dot(value_t, pp, preferred_element_type=F32) + jnp.dot(avalue.T, pa, preferred_element_type=F32)).T
        for g in range(2):
            agrads[:, base + HD * g : base + HD * (g + 1)] = adq[ACT * g : ACT * (g + 1)].astype(BF16)
            agrads[:, base + 512 + HD * g : base + 512 + HD * (g + 1)] = aat[ACT * g : ACT * (g + 1)].astype(BF16)

        for g in range(2):
            for b in range(PREF // block):
                rows = slice(b * block, (b + 1) * block)
                first = HD * (2 * h + g)
                query = proj[rows, first : first + HD]
                dout = proj[rows, QW + 2 * KW + first : QW + 2 * KW + first + HD]
                t, w = soft(key, query)
                w = jnp.where(seg_col[...] <= seg_row[:, rows], w, 0.0)
                p = w * (1.0 / jnp.sum(w, 0, keepdims=True))
                gp = dot_last(value, dout)
                inner = jnp.sum(p * gp, 0, keepdims=True)
                s = (p * (gp - inner) * (1.0 - t * t) * SCALE).astype(BF16)
                p = p.astype(BF16)
                dk[...] += jnp.dot(s, query, preferred_element_type=F32)
                dv[...] += jnp.dot(p, dout, preferred_element_type=F32)
                dq = jnp.dot(key_t, s, preferred_element_type=F32).T
                at = jnp.dot(value_t, p, preferred_element_type=F32).T
                grads[rows, base + HD * g : base + HD * (g + 1)] = dq.astype(BF16)
                grads[rows, base + 512 + HD * g : base + 512 + HD * (g + 1)] = at.astype(BF16)
        grads[:, base + 256 : base + 384] = dk[...].astype(BF16)
        grads[:, base + 384 : base + 512] = dv[...].astype(BF16)


def attend(proj, aproj, seg):
    return pl.pallas_call(
        attend_kernel,
        out_shape=(jax.ShapeDtypeStruct((PREF, COLS), BF16), jax.ShapeDtypeStruct((ACT, COLS), BF16)),
        in_specs=[VMEM] * 4,
        out_specs=(VMEM, VMEM),
        scratch_shapes=[pltpu.VMEM((PREF, HD), F32), pltpu.VMEM((PREF, HD), F32)],
        compiler_params=pltpu.CompilerParams(vmem_limit_bytes=48 << 20),
        name="attend",
    )(proj, aproj, seg[None, :], seg[:, None])


def outer_sum(left_rows, right_rows):
    return lax.dot_general(left_rows, right_rows, (((0,), (0,)), ((), ())), preferred_element_type=F32)


def norm_back(rows, gain, upstream):
    widened = rows.astype(F32)
    inverse = lax.rsqrt(jnp.mean(widened * widened, -1, keepdims=True) + EPSILON)
    normed = widened * inverse
    scaled = upstream * gain
    return (inverse * (scaled - normed * jnp.mean(scaled * normed, -1, keepdims=True))).astype(BF16)


def columns(grads, what):
    first, width = {"q": (0, 256), "k": (256, 128), "v": (384, 128), "o": (512, 256)}[what]
    return jnp.concatenate([grads[:, HALF * h + first : HALF * h + first + width] for h in range(2)], 1)


def per_device(prefix_in, action_in, segment_ids, gain_prefix, gain_action, query_prefix, key_prefix, value_prefix,
               out_prefix, query_action, key_action, value_action, out_action, cot_prefix, cot_action):
    proj, aproj, g_norm, g_cot, s_norm, s_cot, a_norm, sa_norm, sa_cot = gather_and_project(
        prefix_in, cot_prefix, gain_prefix, action_in, cot_action, gain_action, query_prefix, key_prefix,
        value_prefix, out_prefix, query_action, key_action, value_action, out_action)
    order = slot_order()
    seg = segment_ids.reshape(SLOTS, ROWS)[order].reshape(PREF)
    grads, agrads = attend(proj.reshape(PREF, COLS), aproj, seg)
    rows, cots = g_norm.reshape(PREF, D), g_cot.reshape(PREF, D)
    terms = [outer_sum(cots if w == "o" else rows, columns(grads, w)) for w in "qkvo"]
    terms += [outer_sum(cot_action if w == "o" else a_norm, columns(agrads, w)) for w in "qkvo"]
    out = [lax.psum_scatter(t.astype(BF16), "dp", scatter_dimension=0, tiled=True) for t in terms]
    up = sum(dot_last(columns(grads, w), m) for w, m in zip("qkv", (query_prefix, key_prefix, value_prefix)))
    aup = sum(dot_last(columns(agrads, w), m) for w, m in zip("qkv", (query_action, key_action, value_action)))
    up = up.astype(BF16).reshape(SLOTS, ROWS, D)[jnp.argsort(order)].reshape(PREF, D)
    own = lax.psum_scatter(up, "tensor", scatter_dimension=0, tiled=True).astype(F32)
    total = lax.psum(aup.astype(BF16), "tensor").astype(F32)
    return (norm_back(prefix_in, gain_prefix, own), norm_back(action_in, gain_action, total), *out)


def solution(mesh):
    rows, sample, cols = P(("dp", "tensor"), None), P("dp", None), P(None, "tensor")
    in_specs = (rows, sample, sample, P(), P()) + (cols,) * 8 + (rows, sample)
    out_specs = (rows, sample) + (P("dp", "tensor"),) * 8
    return jax.shard_map(per_device, mesh=mesh, in_specs=in_specs, out_specs=out_specs, check_vma=False)
```

time: 1080 us -> 901 us (0.83); the launches traced: 1060 us -> 900 us
  waiting for transfers between devices: 897 us -> 721 us
  Pallas kernels: 0 us -> 83.8 us
  matrix products: 124 us -> 52.3 us
    all_gather x2 -> x0, waiting for transfers between devices: 172 us -> none  [the longest x1 92.5 us: per_device(): lax.all_gather(pre_normed, 'tensor', axis=0, tiled=True)]
    unnamed x14 -> x11, waiting for transfers between devices: 163 us -> 74.6 us
    reduce_scatter x7 -> x8, waiting for transfers between devices: 555 us -> 643 us  [the longest x7 539 us: per_device(): lax.psum_scatter(t.astype(BF16), 'dp', scatter_dimension=0, tiled=True)]
    pallas_call x0 -> x2, Pallas kernels: none -> 83.8 us  [the longest x1 77.1 us: gather_and_project(): pl.pallas_call(gather_kernel, out_shape=(jax.ShapeDtypeStruct((SLOTS, ROW...]
    dot_general x26 -> x6, matrix products: 94.3 us -> 22.4 us  [dot_last(): lax.dot_general(a, b, (((1,), (1,)), ((), ())), preferred_element_type=F32)]
  transfers between devices with their start and end apart: 12 -> 10, of which waited for: 12 -> 10; matrix products, arithmetic and copies ran while one was open for 9% -> 8% of each run, Pallas kernels for 0% -> 0%
where the time goes in v1:
time: 901 us; the launch traced here: 900 us
  waiting for transfers between devices  721 us (80%)
  Pallas kernels  83.8 us (9%)
  matrix products  52.3 us (6%)
  local copies, waits for them, and re-layouts  18 us (2%)
  between operations  14.4 us (2%)
  other arithmetic  9.92 us (1%)
    reduce_scatter x7, waiting for transfers between devices, per_device(): lax.psum_scatter(t.astype(BF16), 'dp', scatter_dimension=0, tiled=True)  539 us
    reduce_scatter x1, waiting for transfers between devices, per_device(): lax.psum_scatter(up, 'tensor', scatter_dimension=0, tiled=True).astype(F32)  104 us
    pallas_call x1, Pallas kernels, gather_and_project(): pl.pallas_call(gather_kernel, out_shape=(jax.ShapeDtypeStruct((SLOTS, ROW...  77.1 us
    unnamed x11, waiting for transfers between devices  74.6 us
    dot_general x8, matrix products, outer_sum(): lax.dot_general(left_rows, right_rows, (((0,), (0,)), ((), ())), preferre...  29.9 us
    dot_general x6, matrix products, dot_last(): lax.dot_general(a, b, (((1,), (1,)), ((), ())), preferred_element_type=F32)  22.4 us
  transfers between devices with their start and end apart: 10, of which 10 were waited for; matrix products, arithmetic and copies ran while one was open for 8% of the time, Pallas kernels for 0%

profile of v1, /device:TPU:1, one launch (start us, length us, event | category | flops | bytes accessed | tf_op | source)
XLA Modules:
  0.0 900.0 jit_solution(8340878421651843182)
XLA Ops:
  7.4 0.5 broadcast.96
  7.9 1.3 reduce.3
  9.3 0.6 gather_fusion
  10.2 1.3 broadcast_in_dim.6.gain
  11.5 77.1 %gather_and_project.1 = (bf16[8,64,1536]{2,1,0:T(8,128)(2,1)}, bf16[48,1536]{1,0:T(8,128)(2,1)}, bf16[8,64,4608]{2,1,0:T(8,128)(2,1)}, bf16[8,64,4608]{2,1,0:T(8...) custom-call(bf16[64,4608]{1,0:T(8,128)(2,1)} %pin.1, ...), custom_call_target="tpu_custom_call" | custom-call | tf_op jit(solution)/shard_map/gather_and_project/pallas_call | solution.py:206
  88.6 1.4 copy-done
  90.0 0.9 copy-done.1
  90.9 6.7 attend.1
  97.7 0.4 fusion.25
  98.1 0.4 fusion.26
  98.6 1.4 fusion.2
  100.0 0.2 reduce-scatter.12.cloned.1.call-start
  100.2 0.9 fusion.42
  101.2 0.9 copy-done.3
  102.1 5.1 fusion.21
  107.2 5.1 fusion.20
  112.3 0.6 stack.62
  112.9 0.5 iota.4
  113.4 1.6 sort.17
  115.0 10.0 %add_convert_fusion = bf16[512,4608]{1,0:T(8,128)(2,1)} fusion(f32[512,4608]{1,0:T(8,128)} %fusion.20, f32[512,4608]{1,0:T(8,128)} %fusion.21, bf16[4608,256]{1,0:T(8,128)(2,1)S(1)} %copy-done.2, bf16[512,128]{1,0:T(8,128)(2,1)S(1)} %get-tuple-element.61, bf16[512,128]{1,0:T(8,128)(2,1)S(1)} %get-tuple-element.60), kind=kOutput, calls=%fused_computation.2 | convolution fusion | flops 1215561728 | bytes 26214400 | tf_op jit(solution)/shard_map/dot_general | solution.py:228
  125.0 5.4 gather_fusion.1
  130.5 0.9 copy-done.9
  131.4 1.5 convolution_convert_fusion.7
  132.9 1.5 convolution_convert_fusion.6
  134.5 2.1 convolution_convert_fusion.5
  136.7 0.7 fusion
  137.4 2.5 copy.30
  140.0 5.2 convolution_convert_fusion.2
  145.3 5.3 convolution_convert_fusion.3
  150.7 6.8 convolution_convert_fusion
  157.5 0.3 reduce-scatter.14.cloned.1.call-start
  157.8 6.8 convolution_convert_fusion.1
  164.6 0.9 copy-done.8
  165.8 0.2 fusion.9
  166.0 2.9 all-reduce.2.cloned.1.call-done
  168.9 1.2 fusion.15
  170.1 1.7 fusion.18
  171.8 104.3 %reduce-scatter.12.cloned.1.call-done = bf16[64,4608]{1,0:T(8,128)(2,1)} async-done(((bf16[512,4608]{1,0:T(8,128)(2,1)}), bf16[64,4608]{1,0:T(8,128)(2,1)}) %reduce-scatter.12.cloned.1.call-update) | async-done | bytes 589840 | tf_op jit(solution)/shard_map/reduce_scatter | solution.py:336
  276.1 1.4 fusion.5
  277.6 2.2 fusion.8
  279.8 67.3 %reduce-scatter.24.cloned.1.call-done = bf16[128,256]{1,0:T(8,128)(2,1)} async-done(((bf16[2048,256]{1,0:T(8,128)(2,1)}), bf16[128,256]{1,0:T(8,128)(2,1)}) %reduce-scatter.24.cloned.1.call-update) | async-done | bytes 65552 | tf_op jit(solution)/shard_map/reduce_scatter | solution.py:332
  347.1 70.2 %reduce-scatter.26.cloned.1.call-done = bf16[128,256]{1,0:T(8,128)(2,1)} async-done(((bf16[2048,256]{1,0:T(8,128)(2,1)}), bf16[128,256]{1,0:T(8,128)(2,1)}) %reduce-scatter.26.cloned.1.call-update) | async-done | bytes 65552 | tf_op jit(solution)/shard_map/reduce_scatter | solution.py:332
  417.3 74.9 %reduce-scatter.22.cloned.1.call-done = bf16[128,512]{1,0:T(8,128)(2,1)} async-done(((bf16[2048,512]{1,0:T(8,128)(2,1)}), bf16[128,512]{1,0:T(8,128)(2,1)}) %reduce-scatter.22.cloned.1.call-update) | async-done | bytes 131088 | tf_op jit(solution)/shard_map/reduce_scatter | solution.py:332
  492.1 74.4 %reduce-scatter.28.cloned.1.call-done = bf16[128,512]{1,0:T(8,128)(2,1)} async-done(((bf16[2048,512]{1,0:T(8,128)(2,1)}), bf16[128,512]{1,0:T(8,128)(2,1)}) %reduce-scatter.28.cloned.1.call-update) | async-done | bytes 131088
  566.5 76.6 %reduce-scatter.18.cloned.1.call-done = bf16[288,256]{1,0:T(8,128)(2,1)} async-done(((bf16[4608,256]{1,0:T(8,128)(2,1)}), bf16[288,256]{1,0:T(8,128)(2,1)}) %reduce-scatter.18.cloned.1.call-update) | async-done | bytes 147472 | tf_op jit(solution)/shard_map/reduce_scatter | solution.py:332
  643.2 76.0 %reduce-scatter.16.cloned.1.call-done = bf16[288,256]{1,0:T(8,128)(2,1)} async-done(((bf16[4608,256]{1,0:T(8,128)(2,1)}), bf16[288,256]{1,0:T(8,128)(2,1)}) %reduce-scatter.16.cloned.1.call-update) | async-done | bytes 147472 | tf_op jit(solution)/shard_map/reduce_scatter | solution.py:332
  719.2 87.8 %reduce-scatter.20.cloned.1.call-done = bf16[288,512]{1,0:T(8,128)(2,1)} async-done(((bf16[4608,512]{1,0:T(8,128)(2,1)}), bf16[288,512]{1,0:T(8,128)(2,1)}) %reduce-scatter.20.cloned.1.call-update) | async-done | bytes 294928 | tf_op jit(solution)/shard_map/reduce_scatter | solution.py:332
  807.0 86.1 %reduce-scatter.14.cloned.1.call-done = bf16[288,512]{1,0:T(8,128)(2,1)} async-done(((bf16[4608,512]{1,0:T(8,128)(2,1)}), bf16[288,512]{1,0:T(8,128)(2,1)}) %reduce-scatter.14.cloned.1.call-update) | async-done | bytes 294928 | tf_op jit(solution)/shard_map/reduce_scatter | solution.py:332
  (66 shorter events, 1.4 us)
Async XLA Ops:
  7.2 161.7 %all-reduce.2.cloned.1.call-start = ((), (), s32[]{:S(2)}) async-start(), calls=%async_computation.10 | async-start | bytes 393216 | tf_op jit(solution)/shard_map/psum | solution.py:337
  11.5 86.2 %copy-start.6 = (bf16[2048,256]{1,0:T(8,128)(2,1)S(1)}, bf16[2048,256]{1,0:T(8,128)(2,1)}, u32[]{:S(2)}) copy-start(bf16[2048,256]{1,0:T(8,128)(2,1)} %av.1) | copy-start | bytes 3145732
  11.5 86.6 %copy-start.7 = (bf16[2048,256]{1,0:T(8,128)(2,1)S(1)}, bf16[2048,256]{1,0:T(8,128)(2,1)}, u32[]{:S(2)}) copy-start(bf16[2048,256]{1,0:T(8,128)(2,1)} %ak.1) | copy-start | bytes 3145732
  11.5 87.0 %copy-start.5 = (bf16[2048,512]{1,0:T(8,128)(2,1)S(1)}, bf16[2048,512]{1,0:T(8,128)(2,1)}, u32[]{:S(2)}) copy-start(bf16[2048,512]{1,0:T(8,128)(2,1)} %aq.1) | copy-start | bytes 6291460
  88.6 1.4 copy-start
  90.0 0.9 copy-start.1
  100.0 176.1 %reduce-scatter.12.cloned.1.call-start = ((), (), s32[]{:S(2)}) async-start(), calls=%async_computation.9 | async-start | bytes 5308416 | tf_op jit(solution)/shard_map/reduce_scatter | solution.py:336
  100.2 1.9 copy-start.3
  101.1 6.1 slice-start
  102.1 5.1 slice-start.1
  107.2 7.9 copy-start.2
  115.0 10.0 %copy-start.15 = (s32[8]{0:T(128)S(1)}, s32[8]{0:T(128)}, u32[]{:S(2)}) copy-start(s32[8]{0:T(128)} %get-tuple-element.21) | copy-start | bytes 100
  130.5 0.9 copy-start.9
  130.5 216.6 %reduce-scatter.24.cloned.1.call-start = ((), (), s32[]{:S(2)}) async-start(), calls=%async_computation.16 | async-start | bytes 1114112 | tf_op jit(solution)/shard_map/reduce_scatter | solution.py:332
  132.8 3.8 copy-start.10
  132.9 284.4 %reduce-scatter.26.cloned.1.call-start = ((), (), s32[]{:S(2)}) async-start(), calls=%async_computation.17 | async-start | bytes 1114112 | tf_op jit(solution)/shard_map/reduce_scatter | solution.py:332
  134.4 357.7 %reduce-scatter.22.cloned.1.call-start = ((), (), s32[]{:S(2)}) async-start(), calls=%async_computation.15 | async-start | bytes 2228224 | tf_op jit(solution)/shard_map/reduce_scatter | solution.py:332
  136.6 429.9 %reduce-scatter.28.cloned.1.call-start = ((), (), s32[]{:S(2)}) async-start(), calls=%async_computation.18 | async-start | bytes 2228224
  139.9 503.2 %reduce-scatter.18.cloned.1.call-start = ((), (), s32[]{:S(2)}) async-start(), calls=%async_computation.13 | async-start | bytes 2506752 | tf_op jit(solution)/shard_map/reduce_scatter | solution.py:332
  145.2 5.5 copy-start.11
  145.2 5.5 copy-start.12
  145.2 574.0 %reduce-scatter.16.cloned.1.call-start = ((), (), s32[]{:S(2)}) async-start(), calls=%async_computation.12 | async-start | bytes 2506752 | tf_op jit(solution)/shard_map/reduce_scatter | solution.py:332
  150.6 656.4 %reduce-scatter.20.cloned.1.call-start = ((), (), s32[]{:S(2)}) async-start(), calls=%async_computation.14 | async-start | bytes 5013504 | tf_op jit(solution)/shard_map/reduce_scatter | solution.py:332
  157.5 735.6 %reduce-scatter.14.cloned.1.call-start = ((), (), s32[]{:S(2)}) async-start(), calls=%async_computation.11 | async-start | bytes 5013504 | tf_op jit(solution)/shard_map/reduce_scatter | solution.py:332
  164.6 0.9 copy-start.8
  164.6 1.2 copy-start.4
  164.6 4.3 copy-start.14
  164.6 111.5 %copy-start.13 = (f32[4608]{0:T(1024)S(1)}, f32[4608]{0:T(1024)}, u32[]{:S(2)}) copy-start(f32[4608]{0:T(1024)} %param.18) | copy-start | bytes 55300
Sparse Core Ops, SparseCore 0:
  100.1 68.7 all-reduce.1
  171.5 104.6 reduce-scatter.11
  280.9 66.0 reduce-scatter.23
  351.3 65.9 reduce-scatter.25
  422.1 70.0 reduce-scatter.21
  496.4 70.0 reduce-scatter.27
  571.6 71.4 reduce-scatter.17
  647.7 71.4 reduce-scatter.15
  724.4 82.4 reduce-scatter.19
  811.5 81.5 reduce-scatter.13

commit v2 on v1

--- a/solution.py
+++ b/solution.py
@@ -301,8 +301,18 @@
     )(proj, aproj, seg[None, :], seg[:, None])
 
 
-def outer_sum(left_rows, right_rows):
-    return lax.dot_general(left_rows, right_rows, (((0,), (0,)), ((), ())), preferred_element_type=F32)
+SHARE = 416
+PRE, ACTS = 288, 128
+Z_PRE, Z_ACT = 4 * PRE, 4 * ACTS
+LHS_TILE = 384
+UP_TILE = 512
+
+
+def add(*terms):
+    total = terms[0].astype(F32)
+    for term in terms[1:]:
+        total = total + term.astype(F32)
+    return total
 
 
 def norm_back(rows, gain, upstream):
@@ -313,9 +323,267 @@
     return (inverse * (scaled - normed * jnp.mean(scaled * normed, -1, keepdims=True))).astype(BF16)
 
 
-def columns(grads, what):
-    first, width = {"q": (0, 256), "k": (256, 128), "v": (384, 128), "o": (512, 256)}[what]
-    return jnp.concatenate([grads[:, HALF * h + first : HALF * h + first + width] for h in range(2)], 1)
+def sum_kernel(
+    g_norm, g_cot, s_norm, s_cot, a_norm, acot, sa_norm, sa_cot, grads, agrads, pin, gain, ain, again,
+    wq, wk, wv, aq, ak, av,
+    pgrad, agrad, final,
+    left_v, act_v, right_v, aright_v, w_v, part, z1_v, z2_v, y_v, done_v, up_v, u1_v, u2_v, uy_v, aup_v, ay_v, ax_v,
+    load_sem, w_sem, ex_send, ex_recv, z1_send, z1_recv, z2_send, z2_recv, y_send, y_recv, f_send, f_recv, f_local,
+    u1_send, u1_recv, u2_send, u2_recv, uy_send, uy_recv, ay_send, ay_recv, ax_send, ax_recv,
+):
+    d = lax.axis_index("dp")
+    z, yh, core = lax.div(d, 4), lax.rem(lax.div(d, 2), 2), lax.rem(d, 2)
+    steps = (2, 1, -1, 0)
+    z_of = [lax.rem(z + s + 4, 4) for s in steps]
+
+    loads = {}
+    for r in range(4):
+        for a, pair in enumerate(((g_norm, s_norm), (g_cot, s_cot))):
+            cols = pl.ds(pl.multiple_of(z_of[r] * Z_PRE, 128), Z_PRE)
+            loads[a, r] = [
+                pltpu.make_async_copy(
+                    ref.at[:, cols], left_v.at[a, r, pl.ds(PREF * i, PREF)], load_sem.at[a, r, i])
+                for i, ref in enumerate(pair)
+            ]
+    for key in ((0, 0), (0, 1), (0, 2), (1, 0), (0, 3), (1, 1), (1, 2), (1, 3)):
+        for copy in loads[key]:
+            copy.start()
+
+    def w_copies(refs, t, slot):
+        rows = pl.ds(pl.multiple_of(t * UP_TILE, UP_TILE), UP_TILE)
+        copies = []
+        for h in range(2):
+            for j, (ref, width, first) in enumerate(zip(refs, (256, 128, 128), (0, 256, 384))):
+                copies.append(pltpu.make_async_copy(
+                    ref.at[rows, pl.ds(width * h, width)],
+                    w_v.at[slot, :, pl.ds(UP_TILE * h + first, width)],
+                    w_sem.at[slot, 3 * h + j]))
+        return copies
+
+    z_right, z_left, across, twin = z_step(1), z_step(-1), y_high(), sibling()
+    x_right, x_left, x_far, y_near = x_step(1), x_step(-1), x_step(2), y_low()
+    greet((z_right, z_left, across, twin, x_right, x_left, x_far, y_near))
+
+    mine = pl.ds(pl.multiple_of(core * HALF, HALF), HALF)
+    theirs = pl.ds(pl.multiple_of((1 - core) * HALF, HALF), HALF)
+    exchange = [
+        remote(grads.at[:, theirs], right_v.at[pl.ds(PREF, PREF)], ex_send.at[0], ex_recv.at[0], twin),
+        remote(agrads.at[:, theirs], aright_v.at[pl.ds(ACT, ACT)], ex_send.at[1], ex_recv.at[1], twin),
+    ]
+    for copy in exchange:
+        copy.start()
+    right_v[0:PREF] = grads[:, mine]
+    aright_v[0:ACT] = agrads[:, mine]
+    act_v[0, 0:ACT] = a_norm[...]
+    act_v[0, ACT : 2 * ACT] = sa_norm[...]
+    act_v[1, 0:ACT] = acot[...]
+    act_v[1, ACT : 2 * ACT] = sa_cot[...]
+
+    loaded = set()
+
+    def weight_grad(g, r):
+        a = 0 if g < 2 else 1
+        if (a, r) not in loaded:
+            loaded.add((a, r))
+            for copy in loads[a, r]:
+                copy.wait()
+        cols = slice(256 * g, 256 * (g + 1))
+        for t in range(Z_PRE // LHS_TILE):
+            low, high = t * LHS_TILE, (t + 1) * LHS_TILE
+            out = lax.dot_general(
+                left_v[a, r, :, low:high], right_v[:, cols], (((0,), (0,)), ((), ())), preferred_element_type=F32
+            ).astype(BF16)
+            for share in range(4):
+                first, last = max(low, PRE * share), min(high, PRE * (share + 1))
+                if first < last:
+                    part[g, r, share // 2, share % 2, first - PRE * share : last - PRE * share] = (
+                        out[first - low : last - low])
+        out = lax.dot_general(
+            act_v[a, :, pl.ds(pl.multiple_of(z_of[r] * Z_ACT, Z_ACT), Z_ACT)], aright_v[:, cols],
+            (((0,), (0,)), ((), ())), preferred_element_type=F32,
+        ).astype(BF16)
+        for share in range(4):
+            part[g, r, share // 2, share % 2, PRE:SHARE] = out[ACTS * share : ACTS * (share + 1)]
+
+    z1 = [
+        [remote(part.at[g, 0, i], z1_v.at[g, i], z1_send.at[g, i], z1_recv.at[g, i], (z_right, z_left)[i])
+         for i in range(2)] for g in range(3)
+    ]
+    z2 = [
+        [[remote(part.at[g, 1 + i, y], z2_v.at[g, i, y], z2_send.at[g, i, y], z2_recv.at[g, i, y],
+                 (z_right, z_left)[i]) for y in range(2)] for i in range(2)] for g in range(3)
+    ]
+    ys = [remote(part.at[g, 3, 1 - yh], y_v.at[g], y_send.at[g], y_recv.at[g], across) for g in range(3)]
+    outs = [
+        remote(done_v.at[g, 1 - core], final.at[core, g], f_send.at[g], f_recv.at[g], twin) for g in range(3)
+    ]
+    kept = [pltpu.make_async_copy(done_v.at[g, core], final.at[core, g], f_local.at[g]) for g in range(3)]
+
+    def z_first(g):
+        weight_grad(g, 0)
+        for copy in z1[g]:
+            copy.start()
+
+    def z_raw(g):
+        weight_grad(g, 1)
+        z2[g][0][1].start()
+        weight_grad(g, 2)
+        z2[g][1][0].start()
+
+    def z_second(g):
+        for i in range(2):
+            z1[g][i].wait_recv()
+            part[g, 1 + i, i] = add(part[g, 1 + i, i], z1_v[g, i]).astype(BF16)
+            z2[g][i][i].start()
+
+    def y_first(g):
+        for i in range(2):
+            for y in range(2):
+                z2[g][i][y].wait_recv()
+        y = 1 - yh
+        part[g, 3, y] = add(part[g, 3, y], z2_v[g, 0, y], z2_v[g, 1, y]).astype(BF16)
+        ys[g].start()
+
+    def finish(g):
+        ys[g].wait_recv()
+        done_v[g] = add(part[g, 3, yh], z2_v[g, 0, yh], z2_v[g, 1, yh], y_v[g]).astype(BF16)
+        outs[g].start()
+        kept[g].start()
+
+    def up_loop(refs, count, use):
+        def step(t, carry):
+            slot = lax.rem(t, 2)
+
+            @pl.when(t + 1 < count)
+            def _():
+                for copy in w_copies(refs, t + 1, 1 - slot):
+                    copy.start()
+
+            for copy in w_copies(refs, t, slot):
+                copy.wait()
+            use(t, slot)
+            return carry
+
+        for copy in w_copies(refs, 0, 0):
+            copy.start()
+        lax.fori_loop(0, count, step, 0)
+
+    def through(cots, slot):
+        return dot_last(cots[:, 0:UP_TILE], w_v[slot, :, 0:UP_TILE]) + dot_last(
+            cots[:, HALF : HALF + UP_TILE], w_v[slot, :, UP_TILE : 2 * UP_TILE])
+
+    def use_pre(t, slot):
+        cols = pl.ds(pl.multiple_of(t * UP_TILE, UP_TILE), UP_TILE)
+        up_v[:, :, cols] = through(grads, slot).astype(BF16).reshape(SLOTS, ROWS, UP_TILE)
+
+    def use_act(t, slot):
+        cols = pl.ds(pl.multiple_of(t * UP_TILE, UP_TILE), UP_TILE)
+        aup_v[:, cols] = through(agrads, slot).astype(BF16)
+
+    u1 = [
+        remote(up_v.at[4], u1_v.at[0], u1_send.at[0], u1_recv.at[0], x_right),
+        remote(up_v.at[7], u1_v.at[1], u1_send.at[1], u1_recv.at[1], x_left),
+    ]
+    u2 = [
+        remote(up_v.at[s], u2_v.at[i], u2_send.at[i], u2_recv.at[i], device)
+        for i, (s, device) in enumerate(((3, x_right), (6, x_right), (2, x_left), (5, x_left)))
+    ]
+    uy = remote(up_v.at[1], uy_v, uy_send.at[0], uy_recv.at[0], y_near)
+    ay = remote(aup_v, ay_v, ay_send.at[0], ay_recv.at[0], y_near)
+    ax = [
+        remote(ax_v.at[0], ax_v.at[1 + i], ax_send.at[i], ax_recv.at[i], device)
+        for i, device in enumerate((x_right, x_left, x_far))
+    ]
+
+    for copy in exchange:
+        copy.wait_recv()
+    z_first(0)
+    z_raw(0)
+    z_first(1)
+    up_loop((aq, ak, av), DA // UP_TILE, use_act)
+    ay.start()
+    up_loop((wq, wk, wv), D // UP_TILE, use_pre)
+    for copy in u1:
+        copy.start()
+    u2[1].start()
+    u2[2].start()
+    z_second(0)
+    z_raw(1)
+    z_first(2)
+    weight_grad(0, 3)
+    ay.wait_recv()
+    ax_v[0] = add(aup_v[...], ay_v[...]).astype(BF16)
+    for copy in ax:
+        copy.start()
+    for i, s in ((0, 3), (1, 5)):
+        u1[i].wait_recv()
+        up_v[s] = add(up_v[s], u1_v[i]).astype(BF16)
+    u2[0].start()
+    u2[3].start()
+    z_second(1)
+    z_raw(2)
+    weight_grad(1, 3)
+    weight_grad(2, 3)
+    y_first(0)
+    z_second(2)
+    for copy in ax:
+        copy.wait_recv()
+    agrad[...] = norm_back(ain[...], again[...], add(ax_v[0], ax_v[3]) + add(ax_v[1], ax_v[2]))
+    for copy in u2:
+        copy.wait_recv()
+    up_v[1] = add(up_v[1], u2_v[1], u2_v[3]).astype(BF16)
+    uy.start()
+    finish(0)
+    y_first(1)
+    uy.wait_recv()
+    pgrad[...] = norm_back(pin[...], gain[...], add(up_v[0], u2_v[0], u2_v[2], uy_v[...]))
+    finish(1)
+    y_first(2)
+    finish(2)
+
+    for copy in (*exchange, *u1, *u2, uy, ay, *ax):
+        copy.wait_send()
+    for g in range(3):
+        for i in range(2):
+            z1[g][i].wait_send()
+            for y in range(2):
+                z2[g][i][y].wait_send()
+        ys[g].wait_send()
+        outs[g].wait()
+        kept[g].wait()
+
+
+def sum_everything(g_norm, g_cot, s_norm, s_cot, *rest):
+    wide = tuple(m.reshape(PREF, D) for m in (g_norm, g_cot, s_norm, s_cot))
+    dma = pltpu.SemaphoreType.DMA
+    share = (2, SHARE, 256)
+    row = (ROWS, D)
+
+    def held(*shape):
+        return pltpu.VMEM(shape, BF16)
+
+    return pl.pallas_call(
+        sum_kernel,
+        out_shape=(
+            jax.ShapeDtypeStruct(row, BF16), jax.ShapeDtypeStruct((ACT, DA), BF16),
+            jax.ShapeDtypeStruct((2, 3, SHARE, 256), BF16),
+        ),
+        in_specs=[ANY] * 4 + [VMEM] * 10 + [ANY] * 6,
+        out_specs=(VMEM, VMEM, ANY),
+        scratch_shapes=[
+            held(2, 4, 2 * PREF, Z_PRE), held(2, 2 * ACT, DA), held(2 * PREF, HALF), held(2 * ACT, HALF),
+            held(2, UP_TILE, 2 * UP_TILE), held(3, 4, 2, *share), held(3, 2, *share), held(3, 2, 2, *share),
+            held(3, *share), held(3, *share), held(SLOTS, *row), held(2, *row), held(4, *row), held(*row),
+            held(ACT, DA), held(ACT, DA), held(4, ACT, DA),
+            dma((2, 4, 2)), dma((2, 6)), dma((2,)), dma((2,)), dma((3, 2)), dma((3, 2)), dma((3, 2, 2)), dma((3, 2, 2)),
+            dma((3,)), dma((3,)), dma((3,)), dma((3,)), dma((3,)),
+            dma((2,)), dma((2,)), dma((4,)), dma((4,)), dma((1,)), dma((1,)), dma((1,)), dma((1,)), dma((3,)), dma((3,)),
+        ],
+        compiler_params=pltpu.CompilerParams(
+            collective_id=1, has_side_effects=True, vmem_limit_bytes=62 << 20
+        ),
+        name="sum_everything",
+    )(*wide, *rest)
 
 
 def per_device(prefix_in, action_in, segment_ids, gain_prefix, gain_action, query_prefix, key_prefix, value_prefix,
@@ -323,19 +591,21 @@
     proj, aproj, g_norm, g_cot, s_norm, s_cot, a_norm, sa_norm, sa_cot = gather_and_project(
         prefix_in, cot_prefix, gain_prefix, action_in, cot_action, gain_action, query_prefix, key_prefix,
         value_prefix, out_prefix, query_action, key_action, value_action, out_action)
-    order = slot_order()
-    seg = segment_ids.reshape(SLOTS, ROWS)[order].reshape(PREF)
+    seg = segment_ids.reshape(SLOTS, ROWS)[slot_order()].reshape(PREF)
     grads, agrads = attend(proj.reshape(PREF, COLS), aproj, seg)
-    rows, cots = g_norm.reshape(PREF, D), g_cot.reshape(PREF, D)
-    terms = [outer_sum(cots if w == "o" else rows, columns(grads, w)) for w in "qkvo"]
-    terms += [outer_sum(cot_action if w == "o" else a_norm, columns(agrads, w)) for w in "qkvo"]
-    out = [lax.psum_scatter(t.astype(BF16), "dp", scatter_dimension=0, tiled=True) for t in terms]
-    up = sum(dot_last(columns(grads, w), m) for w, m in zip("qkv", (query_prefix, key_prefix, value_prefix)))
-    aup = sum(dot_last(columns(agrads, w), m) for w, m in zip("qkv", (query_action, key_action, value_action)))
-    up = up.astype(BF16).reshape(SLOTS, ROWS, D)[jnp.argsort(order)].reshape(PREF, D)
-    own = lax.psum_scatter(up, "tensor", scatter_dimension=0, tiled=True).astype(F32)
-    total = lax.psum(aup.astype(BF16), "tensor").astype(F32)
-    return (norm_back(prefix_in, gain_prefix, own), norm_back(action_in, gain_action, total), *out)
+    prefix_grad, action_grad, final = sum_everything(
+        g_norm, g_cot, s_norm, s_cot, a_norm, cot_action, sa_norm, sa_cot, grads, agrads,
+        prefix_in, gain_prefix[None, :], action_in, gain_action[None, :],
+        query_prefix, key_prefix, value_prefix, query_action, key_action, value_action)
+
+    def both(g, rows, cols):
+        return jnp.concatenate([final[0, g, rows, cols], final[1, g, rows, cols]], 1)
+
+    out = []
+    for rows in (slice(0, PRE), slice(PRE, SHARE)):
+        for g, cols in ((0, slice(0, 256)), (1, slice(0, 128)), (1, slice(128, 256)), (2, slice(0, 256))):
+            out.append(both(g, rows, cols))
+    return (prefix_grad, action_grad, *out)
 
 
 def solution(mesh):

time: 901 us -> 216 us (0.24)
  waiting for transfers between devices: 721 us -> 0 us
  Pallas kernels: 83.8 us -> 198 us
  matrix products: 52.3 us -> 0 us
  between operations: 14.4 us -> 0.77 us
    reduce_scatter x8 -> x0, waiting for transfers between devices: 643 us -> none  [the longest x7 539 us: per_device(): lax.psum_scatter(t.astype(BF16), 'dp', scatter_dimension=0, tiled=True)]
    pallas_call x0 -> x1, Pallas kernels: none -> 114 us  [sum_everything(): pl.pallas_call(sum_kernel, out_shape=(jax.ShapeDtypeStruct(row, BF16), ja...]
    unnamed x11 -> x0, waiting for transfers between devices: 74.6 us -> none
    dot_general x14 -> x0, matrix products: 52.3 us -> none  [the longest x8 29.9 us: outer_sum(): lax.dot_general(left_rows, right_rows, (((0,), (0,)), ((), ())), preferre...]
  transfers between devices with their start and end apart: 10 -> 0, of which waited for: 10 -> 0; matrix products, arithmetic and copies ran while one was open for 8% -> 0% of each run, Pallas kernels for 0% -> 0%
where the time goes in v2:
time: 216 us; the launch traced here: 215 us
  Pallas kernels  198 us (92%)
  local copies, waits for them, and re-layouts  12.5 us (6%)
  other arithmetic  4.34 us (2%)
    pallas_call x1, Pallas kernels, sum_everything(): pl.pallas_call(sum_kernel, out_shape=(jax.ShapeDtypeStruct(row, BF16), ja...  114 us
    pallas_call x1, Pallas kernels, gather_and_project(): pl.pallas_call(gather_kernel, out_shape=(jax.ShapeDtypeStruct((SLOTS, ROW...  77.1 us
    pallas_call x1, Pallas kernels, attend(): pl.pallas_call(attend_kernel, out_shape=(jax.ShapeDtypeStruct((PREF, COLS...  6.72 us
    unnamed x15, local copies, waits for them, and re-layouts  6.15 us

profile of v2, /device:TPU:1, one launch (start us, length us, event | category | flops | bytes accessed | tf_op | source)
XLA Modules:
  0.0 215.3 jit_solution(5520384472731626848)
XLA Ops:
  0.7 0.1 stack.35
  0.8 0.5 broadcast.36
  1.3 1.3 reduce.3
  2.7 0.1 reshape.356
  2.7 0.6 gather_fusion
  3.3 0.1 broadcast_in_dim_reshape.6.seg_row
  3.4 1.3 broadcast_in_dim.4.gain
  4.7 0.2 broadcast_in_dim_reshape.8.seg_col
  4.9 77.1 %gather_and_project.1 = (bf16[8,64,1536]{2,1,0:T(8,128)(2,1)}, bf16[48,1536]{1,0:T(8,128)(2,1)}, bf16[8,64,4608]{2,1,0:T(8,128)(2,1)}, bf16[8,64,4608]{2,1,0:T(8...) custom-call(bf16[64,4608]{1,0:T(8,128)(2,1)} %pin.3, ...), custom_call_target="tpu_custom_call" | custom-call | tf_op jit(solution)/shard_map/gather_and_project/pallas_call | solution.py:206
  82.0 0.0 copy-start.1
  82.0 1.4 copy-done.1
  83.4 0.0 copy-start.3
  83.4 0.9 copy-done.3
  84.4 6.7 %attend.1 = (bf16[512,1536]{1,0:T(8,128)(2,1)S(1)}, bf16[48,1536]{1,0:T(8,128)(2,1)S(1)}) custom-call(bf16[512,1536]{1,0:T(8,128)(2,1)S(1)} %bitcast.48, bf16[48,1536]{1,0:T(8,128)(2,1)S(1)} %copy-done.3, s32[1,512]{1,0:T(1,128)S(1)} %broadcast_in_dim_reshape.6.seg_row, s32[512,1]{1,0:T(8,128)S(1)} %broadcast_in_dim_reshape.8.seg_col), custom_call_target="tpu_custom_call" | custom-call | tf_op jit(solution)/shard_map/attend/pallas_call | solution.py:293
  91.1 0.0 copy-start
  91.1 1.2 copy-done
  92.3 0.0 copy-start.2
  92.3 0.7 copy-done.2
  92.9 113.8 %sum_everything.1 = (bf16[64,4608]{1,0:T(8,128)(2,1)}, bf16[48,2048]{1,0:T(8,128)(2,1)}, bf16[2,3,416,256]{3,2,1,0:T(8,128)(2,1)}) custom-call(bf16[512,4608]{1,0:T(8,128)(2,1)} %bitcast.49, bf16[512,4608]{1,0:T(8,128)(2,1)} %bitcast.50, bf16[512,4608]{1,0:T(8,128)(2,1)} %bitcast.51, bf16[512,4608]{1,0:T(8,128)(2,1)} %bitcast.52, ...), custom_call_target="tpu_custom_call" | custom-call | tf_op jit(solution)/shard_map/sum_everything/pallas_call | solution.py:565
  206.8 0.8 slice_bitcast_fusion.13
  207.6 0.7 pad_maximum_fusion.6
  208.3 1.0 slice_bitcast_fusion.9
  209.2 0.0 copy-start.4
  209.2 0.7 pad_maximum_fusion.4
  209.9 1.0 slice_bitcast_fusion.5
  210.9 0.0 copy-start.5
  211.0 1.2 slice_bitcast_fusion.1
  212.2 0.7 pad_maximum_fusion.2
  212.9 0.9 pad_maximum_fusion
  213.8 0.0 copy-done.4
  213.8 0.8 copy.28
  214.6 0.0 copy-done.5
  214.6 0.7 copy.29
  (2 shorter events, 0.0 us)
Async XLA Ops:
  82.0 1.4 copy-start.1
  83.4 0.9 copy-start.3
  91.1 1.2 copy-start
  92.3 0.7 copy-start.2
  209.2 4.6 %copy-start.4 = (bf16[64,4608]{1,0:T(8,128)(2,1)S(1)}, bf16[64,4608]{1,0:T(8,128)(2,1)}, u32[]{:S(2)}) copy-start(bf16[64,4608]{1,0:T(8,128)(2,1)} %get-tuple-element.72) | copy-start | bytes 1769476
  210.9 3.6 %copy-start.5 = (bf16[48,2048]{1,0:T(8,128)(2,1)S(1)}, bf16[48,2048]{1,0:T(8,128)(2,1)}, u32[]{:S(2)}) copy-start(bf16[48,2048]{1,0:T(8,128)(2,1)} %get-tuple-element.73) | copy-start | bytes 589828

commit v3 on v2

v3 whole, which is shorter than its diff:
```python
import functools
import math

import jax
import jax.numpy as jnp
from jax import lax
from jax.experimental import pallas as pl
from jax.experimental.pallas import tpu as pltpu
from jax.sharding import PartitionSpec as P

D = 4608
DA = 2048
H = 32
HD = 128
ROWS = 64
ACT = 48
SLOTS = 8
PREF = SLOTS * ROWS
QW, KW = 512, 256
COLS = 2 * QW + 2 * KW
HALF = COLS // 2
TILE = 256
EPSILON = 1e-06
SOFT_CAP = 50.0
SCALE = 1.0 / math.sqrt(D // H)
MESH = pl.DeviceIdType.MESH
BF16, F32 = jnp.bfloat16, jnp.float32
VMEM = pl.BlockSpec(memory_space=pltpu.VMEM)
ANY = pl.BlockSpec(memory_space=pl.ANY)


def x_step(k):
    return lax.axis_index("dp"), lax.rem(lax.axis_index("tensor") + 2 * k + 8, 8)


def z_step(k):
    return lax.rem(lax.axis_index("dp") + 4 * k + 16, 16), lax.axis_index("tensor")


def y_low():
    t = lax.axis_index("tensor")
    return lax.axis_index("dp"), t + 1 - 2 * lax.rem(t, 2)


def y_high():
    d = lax.axis_index("dp")
    return d + 2 - 4 * lax.rem(lax.div(d, 2), 2), lax.axis_index("tensor")


def sibling():
    d = lax.axis_index("dp")
    return d + 1 - 2 * lax.rem(d, 2), lax.axis_index("tensor")


def slot_order():
    t = lax.axis_index("tensor")
    x, y = lax.div(t, 2), lax.rem(t, 2)

    def at(step, row):
        return 2 * lax.rem(x + step + 4, 4) + row

    return [at(0, y), at(0, 1 - y), at(-1, y), at(1, y), at(2, y), at(-1, 1 - y), at(1, 1 - y), at(2, 1 - y)]


def greet(partners, meanwhile):
    barrier = pltpu.get_barrier_semaphore()
    for device in partners:
        pl.semaphore_signal(barrier, inc=1, device_id=device, device_id_type=MESH)
    meanwhile()
    pl.semaphore_wait(barrier, len(partners))


def remote(src, dst, send, recv, device):
    return pltpu.make_async_remote_copy(
        src_ref=src, dst_ref=dst, send_sem=send, recv_sem=recv, device_id=device, device_id_type=MESH
    )


def norm(rows, gain):
    widened = rows.astype(F32)
    inverse = lax.rsqrt(jnp.mean(widened * widened, -1, keepdims=True) + EPSILON)
    return (widened * inverse * gain).astype(BF16)


def dot_last(a, b):
    return lax.dot_general(a, b, (((1,), (1,)), ((), ())), preferred_element_type=F32)


def soft(key_rows, query_rows):
    t = jnp.tanh(dot_last(key_rows, query_rows) * (SCALE / SOFT_CAP))
    return t, jnp.exp(SOFT_CAP * t)


def attend(h, proj, aproj, seg_row, seg_col, grads, agrads, dk, dv):
    block = 256

    def cols(first, width=HD):
        return pl.ds(pl.multiple_of(first, HD), width)

    key = proj[:, :, cols(QW + HD * h)].reshape(PREF, HD)
    value = proj[:, :, cols(QW + KW + HD * h)].reshape(PREF, HD)
    key_t, value_t = key.T, value.T
    base = HALF * h
    akey = aproj[:, cols(QW + HD * h)]
    avalue = aproj[:, cols(QW + KW + HD * h)]

    def two(first):
        return jnp.concatenate([aproj[:, cols(first + HD * (2 * h + g))] for g in range(2)], 0)

    aq, ado = two(0), two(QW + 2 * KW)
    tp, wp = soft(key, aq)
    ta, wa = soft(akey, aq)
    rate = 1.0 / (jnp.sum(wp, 0, keepdims=True) + jnp.sum(wa, 0, keepdims=True))
    pp, pa = wp * rate, wa * rate
    gp, ga = dot_last(value, ado), dot_last(avalue, ado)
    inner = jnp.sum(pp * gp, 0, keepdims=True) + jnp.sum(pa * ga, 0, keepdims=True)
    sp = (pp * (gp - inner) * (1.0 - tp * tp) * SCALE).astype(BF16)
    sa = (pa * (ga - inner) * (1.0 - ta * ta) * SCALE).astype(BF16)
    pp, pa = pp.astype(BF16), pa.astype(BF16)
    dk[...] = jnp.dot(sp, aq, preferred_element_type=F32)
    dv[...] = jnp.dot(pp, ado, preferred_element_type=F32)
    agrads[:, cols(base + 256)] = jnp.dot(sa, aq, preferred_element_type=F32).astype(BF16)
    agrads[:, cols(base + 384)] = jnp.dot(pa, ado, preferred_element_type=F32).astype(BF16)
    adq = (jnp.dot(key_t, sp, preferred_element_type=F32) + jnp.dot(akey.T, sa, preferred_element_type=F32)).T
    aat = (jnp.dot(value_t, pp, preferred_element_type=F32) + jnp.dot(avalue.T, pa, preferred_element_type=F32)).T
    for g in range(2):
        agrads[:, cols(base + HD * g)] = adq[ACT * g : ACT * (g + 1)].astype(BF16)
        agrads[:, cols(base + 512 + HD * g)] = aat[ACT * g : ACT * (g + 1)].astype(BF16)

    for g in range(2):
        for b in range(PREF // block):
            rows = slice(b * block, (b + 1) * block)
            slots = slice(b * block // ROWS, (b + 1) * block // ROWS)
            first = HD * (2 * h + g)
            query = proj[slots, :, cols(first)].reshape(block, HD)
            dout = proj[slots, :, cols(QW + 2 * KW + first)].reshape(block, HD)
            t, w = soft(key, query)
            w = jnp.where(seg_col <= seg_row[:, rows], w, 0.0)
            p = w * (1.0 / jnp.sum(w, 0, keepdims=True))
            gp = dot_last(value, dout)
            inner = jnp.sum(p * gp, 0, keepdims=True)
            s = (p * (gp - inner) * (1.0 - t * t) * SCALE).astype(BF16)
            p = p.astype(BF16)
            dk[...] += jnp.dot(s, query, preferred_element_type=F32)
            dv[...] += jnp.dot(p, dout, preferred_element_type=F32)
            dq = jnp.dot(key_t, s, preferred_element_type=F32).T
            at = jnp.dot(value_t, p, preferred_element_type=F32).T
            grads[rows, cols(base + HD * g)] = dq.astype(BF16)
            grads[rows, cols(base + 512 + HD * g)] = at.astype(BF16)
    grads[:, cols(base + 256)] = dk[...].astype(BF16)
    grads[:, cols(base + 384)] = dv[...].astype(BF16)


def gather_kernel(
    pin, cot, gain, ain, acot, again, seg, wq, wk, wv, wo, aq, ak, av, ao,
    grads, agrads, s_grads, sa_grads, g_norm, g_cot, s_norm, s_cot, a_norm, sa_norm, sa_cot,
    norm_v, cot_v, w_v, aw_v, proj, aproj, dk, dv,
    send, recv, sib_send, sib_recv, local, w_sem, act_send, act_recv,
):
    weights = []
    for i, (ref, first) in enumerate(((aq, 0), (ak, QW), (av, QW + KW), (ao, QW + 2 * KW))):
        weights.append(pltpu.make_async_copy(ref, aw_v.at[:, pl.ds(first, ref.shape[1])], w_sem.at[i]))
    for i, (ref, first) in enumerate(((wq, 0), (wk, QW), (wv, QW + KW), (wo, QW + 2 * KW))):
        weights.append(pltpu.make_async_copy(ref, w_v.at[:, pl.ds(first, ref.shape[1])], w_sem.at[4 + i]))
    for copy in weights:
        copy.start()
    left, right, across, twin = x_step(-1), x_step(1), y_low(), sibling()

    def own_rows():
        cot_v[0] = cot[...]
        norm_v[0] = norm(pin[...], gain[...])

    greet((left, right, across, twin), own_rows)

    arrays = ((norm_v, g_norm, s_norm), (cot_v, g_cot, s_cot))

    def hop(a, src, dst, device):
        held = arrays[a][0]
        return remote(held.at[src], held.at[dst], send.at[a, dst], recv.at[a, dst], device)

    hops = [
        {1: hop(a, 0, 1, across), 2: hop(a, 0, 2, right), 3: hop(a, 0, 3, left),
         4: hop(a, 2, 4, right) if a == 0 else hop(a, 3, 4, left),
         5: hop(a, 1, 5, right), 6: hop(a, 1, 6, left), 7: hop(a, 4, 7, across)}
        for a in range(2)
    ]
    twins = [
        [remote(held.at[s], far.at[s], sib_send.at[a, s], sib_recv.at[a, s], twin) for s in range(SLOTS)]
        for a, (held, _, far) in enumerate(arrays)
    ]
    stores = [
        [pltpu.make_async_copy(held.at[s], near.at[s], local.at[a, s]) for s in range(SLOTS)]
        for a, (held, near, _) in enumerate(arrays)
    ]

    def spread(a, s):
        twins[a][s].start()
        stores[a][s].start()

    right_of = (hops[0][2], hops[1][2])
    left_of = (hops[0][3], hops[1][3])
    right_of[0].start()
    left_of[1].start()
    for a in range(2):
        hops[a][1].start()
    spread(1, 0)
    spread(0, 0)

    a_norm[...] = norm(ain[...], again[...])
    act_twins = [
        remote(a_norm, sa_norm, act_send.at[0], act_recv.at[0], twin),
        remote(acot, sa_cot, act_send.at[1], act_recv.at[1], twin),
    ]
    for copy in act_twins:
        copy.start()
    for copy in weights[:4]:
        copy.wait()

    def act_project(rows, first):
        def step(j, carry):
            cols = pl.ds(pl.multiple_of(j * TILE, TILE), TILE)
            aproj[:, cols] = jnp.dot(rows[...], aw_v[:, cols], preferred_element_type=F32).astype(BF16)
            return carry

        lax.fori_loop(first, first + (4 if first == 0 else 2), step, 0)

    act_project(a_norm, 0)
    act_project(acot, 4)

    def project(held, low, high, first):
        def step(j, carry):
            cols = pl.ds(pl.multiple_of(j * TILE, TILE), TILE)
            rows = held[low:high].reshape((high - low) * ROWS, D)
            out = jnp.dot(rows, w_v[:, cols], preferred_element_type=F32).astype(BF16)
            proj[low:high, :, cols] = out.reshape(high - low, ROWS, TILE)
            return carry

        lax.fori_loop(first, first + (4 if first == 0 else 2), step, 0)

    right_of[0].wait_send()
    right_of[1].start()
    left_of[1].wait_send()
    left_of[0].start()
    hops[0][2].wait_recv()
    hops[0][4].start()
    hops[1][3].wait_recv()
    hops[1][4].start()
    spread(0, 2)
    spread(1, 3)
    for copy in weights[4:]:
        copy.wait()
    for a in range(2):
        hops[a][1].wait_recv()
        spread(a, 1)
    hops[0][4].wait_send()
    hops[0][5].start()
    hops[1][4].wait_send()
    hops[0][6].start()
    for a in range(2):
        hops[a][4].wait_recv()
        hops[a][7].start()
        spread(a, 4)
    right_of[1].wait_send()
    left_of[0].wait_send()
    hops[1][2].wait_recv()
    hops[0][3].wait_recv()
    spread(1, 2)
    spread(0, 3)
    project(norm_v, 0, 4, 0)
    hops[0][5].wait_send()
    hops[1][5].start()
    hops[0][6].wait_send()
    hops[1][6].start()
    project(cot_v, 0, 4, 4)
    for a, first in ((0, 0), (1, 4)):
        for s in (5, 6, 7):
            hops[a][s].wait_recv()
            spread(a, s)
        project(arrays[a][0], 4, 8, first)

    core = lax.rem(lax.axis_index("dp"), 2)
    seg_row = jnp.concatenate([seg[pl.ds(s, 1), :] for s in slot_order()], 1).astype(F32)
    seg_col = jnp.broadcast_to(seg_row, (8, PREF)).T[:, 0:1]
    attend(1 - core, proj, aproj, seg_row, seg_col, grads, agrads, dk, dv)
    theirs = pl.ds(pl.multiple_of((1 - core) * HALF, HALF), HALF)
    act_twins += [
        remote(grads.at[:, theirs], s_grads, act_send.at[2], act_recv.at[2], twin),
        remote(agrads.at[:, theirs], sa_grads, act_send.at[3], act_recv.at[3], twin),
    ]
    for copy in act_twins[2:]:
        copy.start()
    attend(core, proj, aproj, seg_row, seg_col, grads, agrads, dk, dv)
    for a in range(2):
        hops[a][1].wait_send()
        hops[a][7].wait_send()
        for s in range(SLOTS):
            twins[a][s].wait()
            stores[a][s].wait()
    for s in (5, 6):
        hops[1][s].wait_send()
    for copy in act_twins:
        copy.wait()


def gather_and_attend(pin, cot, gain, ain, acot, again, seg, *weights):
    rows = jax.ShapeDtypeStruct((SLOTS, ROWS, D), BF16)
    acts = jax.ShapeDtypeStruct((ACT, DA), BF16)
    dma = pltpu.SemaphoreType.DMA
    return pl.pallas_call(
        gather_kernel,
        out_shape=(
            jax.ShapeDtypeStruct((PREF, COLS), BF16), jax.ShapeDtypeStruct((ACT, COLS), BF16),
            jax.ShapeDtypeStruct((PREF, HALF), BF16), jax.ShapeDtypeStruct((ACT, HALF), BF16),
            rows, rows, rows, rows, acts, acts, acts,
        ),
        in_specs=[VMEM] * 7 + [ANY] * 8,
        out_specs=(VMEM, VMEM, ANY, ANY, ANY, ANY, ANY, ANY, VMEM, ANY, ANY),
        scratch_shapes=[
            pltpu.VMEM((SLOTS, ROWS, D), BF16), pltpu.VMEM((SLOTS, ROWS, D), BF16),
            pltpu.VMEM((D, COLS), BF16), pltpu.VMEM((DA, COLS), BF16),
            pltpu.VMEM((SLOTS, ROWS, COLS), BF16), pltpu.VMEM((ACT, COLS), BF16),
            pltpu.VMEM((PREF, HD), F32), pltpu.VMEM((PREF, HD), F32),
            dma((2, SLOTS)), dma((2, SLOTS)), dma((2, SLOTS)), dma((2, SLOTS)), dma((2, SLOTS)),
            dma((8,)), dma((4,)), dma((4,)),
        ],
        compiler_params=pltpu.CompilerParams(
            collective_id=0, has_side_effects=True, vmem_limit_bytes=60 << 20
        ),
        name="gather_and_attend",
    )(pin, cot, gain[None, :], ain, acot, again[None, :], seg, *weights)


SHARE = 416
PRE, ACTS = 288, 128
Z_PRE, Z_ACT = 4 * PRE, 4 * ACTS
LHS_TILE = 384
UP_TILE = 384
ACT_TILE = 512
HALF_D = D // 2


class Link:
    def __init__(self, window):
        self.window, self.flying = window, []

    def start(self, copy):
        if len(self.flying) == self.window:
            self.flying.pop(0).wait_send()
        copy.start()
        self.flying.append(copy)

    def drain(self):
        for copy in self.flying:
            copy.wait_send()


def add(*terms):
    total = terms[0].astype(F32)
    for term in terms[1:]:
        total = total + term.astype(F32)
    return total


def norm_back(rows, gain, upstream):
    widened = rows.astype(F32)
    inverse = lax.rsqrt(jnp.mean(widened * widened, -1, keepdims=True) + EPSILON)
    normed = widened * inverse
    scaled = upstream * gain
    return (inverse * (scaled - normed * jnp.mean(scaled * normed, -1, keepdims=True))).astype(BF16)


def sum_kernel(
    g_norm, g_cot, s_norm, s_cot, s_grads, a_norm, acot, sa_norm, sa_cot, grads, agrads, sa_grads, pin, gain, ain, again,
    wq, wk, wv, aq, ak, av,
    pgrad, agrad, final,
    left_v, act_v, right_v, aright_v, w_v, part, z1_v, z2_v, h1_v, h2_v, y0_v, y_v, done_v, up_v, u1_v, u2_v, uy_v, aup_v, ay_v, ax_v,
    load_sem, w_sem, ex_sem, z1_send, z1_recv, z2_send, z2_recv, h1_send, h1_recv, h2_send, h2_recv, y0_send, y0_recv, y_send, y_recv, f_send, f_recv, f_local,
    u1_send, u1_recv, u2_send, u2_recv, uy_send, uy_recv, ay_send, ay_recv, ax_send, ax_recv,
):
    d = lax.axis_index("dp")
    z, yh, core = lax.div(d, 4), lax.rem(lax.div(d, 2), 2), lax.rem(d, 2)
    steps = (2, 1, -1, 0)
    z_of = [lax.rem(z + s + 4, 4) for s in steps]

    loads = {}
    for r in range(4):
        for a, pair in enumerate(((g_norm, s_norm), (g_cot, s_cot))):
            cols = pl.ds(pl.multiple_of(z_of[r] * Z_PRE, 128), Z_PRE)
            loads[a, r] = [
                pltpu.make_async_copy(
                    ref.at[:, cols], left_v.at[a, r, pl.ds(PREF * i, PREF)], load_sem.at[a, r, i])
                for i, ref in enumerate(pair)
            ]
    def w_copies(refs, tile, t):
        slot = lax.rem(t, 3)
        rows = pl.ds(pl.multiple_of(t * tile, tile), tile)
        copies = []
        for h in range(2):
            for j, (ref, width, first) in enumerate(zip(refs, (256, 128, 128), (0, 256, 384))):
                copies.append(pltpu.make_async_copy(
                    ref.at[rows, pl.ds(width * h, width)],
                    w_v.at[slot, pl.ds(0, tile), pl.ds(512 * h + first, width)],
                    w_sem.at[slot, 3 * h + j]))
        return copies

    def prime(refs, tile):
        for t in range(2):
            for copy in w_copies(refs, tile, t):
                copy.start()

    prime((aq, ak, av), ACT_TILE)
    z_right, z_left, across, twin = z_step(1), z_step(-1), y_high(), sibling()
    x_right, x_left, x_far, y_near = x_step(1), x_step(-1), x_step(2), y_low()
    mine = pl.ds(pl.multiple_of(core * HALF, HALF), HALF)
    twin_half = pltpu.make_async_copy(s_grads, right_v.at[pl.ds(PREF, PREF)], ex_sem.at[0])
    twin_half.start()
    for key in ((0, 0), (0, 1), (0, 2), (0, 3)):
        for copy in loads[key]:
            copy.start()
    right_v[0:PREF] = grads[:, mine]
    aright_v[0:ACT] = agrads[:, mine]
    aright_v[ACT : 2 * ACT] = sa_grads[...]
    act_v[0, 0:ACT] = a_norm[...]
    act_v[0, ACT : 2 * ACT] = sa_norm[...]
    act_v[1, 0:ACT] = acot[...]
    act_v[1, ACT : 2 * ACT] = sa_cot[...]
    twin_half.wait()

    loaded = set()

    def weight_grad(g, r):
        a = 0 if g < 2 else 1
        if (a, r) not in loaded:
            loaded.add((a, r))
            for copy in loads[a, r]:
                copy.wait()
        cols = slice(256 * g, 256 * (g + 1))
        for t in range(Z_PRE // LHS_TILE):
            low, high = t * LHS_TILE, (t + 1) * LHS_TILE
            out = lax.dot_general(
                left_v[a, r, :, low:high], right_v[:, cols], (((0,), (0,)), ((), ())), preferred_element_type=F32
            ).astype(BF16)
            for share in range(4):
                first, last = max(low, PRE * share), min(high, PRE * (share + 1))
                if first < last:
                    part[g, r, share // 2, share % 2, first - PRE * share : last - PRE * share] = (
                        out[first - low : last - low])
        out = lax.dot_general(
            act_v[a, :, pl.ds(pl.multiple_of(z_of[r] * Z_ACT, Z_ACT), Z_ACT)], aright_v[:, cols],
            (((0,), (0,)), ((), ())), preferred_element_type=F32,
        ).astype(BF16)
        for share in range(4):
            part[g, r, share // 2, share % 2, PRE:SHARE] = out[ACTS * share : ACTS * (share + 1)]

    sides = (z_right, z_left)
    z1 = {g: [
        remote(part.at[g, 0, i], z1_v.at[g - 1, i], z1_send.at[g - 1, i], z1_recv.at[g - 1, i], sides[i])
        for i in range(2)] for g in (1, 2)}
    z2 = {g: [[
        remote(part.at[g, 1 + i, y], z2_v.at[g - 1, i, y], z2_send.at[g - 1, i, y], z2_recv.at[g - 1, i, y], sides[i])
        for y in range(2)] for i in range(2)] for g in (1, 2)}
    ys = {g: remote(part.at[g, 3, 1 - yh], y_v.at[g - 1], y_send.at[g - 1], y_recv.at[g - 1], across) for g in (1, 2)}
    y0 = [remote(part.at[0, r, 1 - yh], y0_v.at[r], y0_send.at[r], y0_recv.at[r], across) for r in range(4)]
    h1 = [remote(part.at[0, 0, yh, i], h1_v.at[i], h1_send.at[i], h1_recv.at[i], sides[i]) for i in range(2)]
    h2 = [[
        remote(part.at[0, 1 + i, yh, c], h2_v.at[i, c], h2_send.at[i, c], h2_recv.at[i, c], sides[i])
        for c in range(2)] for i in range(2)]
    outs = [
        remote(done_v.at[g, 1 - core], final.at[core, g], f_send.at[g], f_recv.at[g], twin) for g in range(3)
    ]
    kept = [pltpu.make_async_copy(done_v.at[g, core], final.at[core, g], f_local.at[g]) for g in range(3)]
    z_links, y_link = (Link(2), Link(2)), Link(2)

    def z_first(g, compute=True):
        if compute:
            weight_grad(g, 0)
        for i in range(2):
            z_links[i].start(z1[g][i])

    def z_raw(g):
        for i in range(2):
            weight_grad(g, 1 + i)
            z_links[i].start(z2[g][i][1 - i])

    def z_second(g):
        for i in range(2):
            z1[g][i].wait_recv()
            part[g, 1 + i, i] = add(part[g, 1 + i, i], z1_v[g - 1, i]).astype(BF16)
            z_links[i].start(z2[g][i][i])

    def y_last(g):
        for i in range(2):
            for y in range(2):
                z2[g][i][y].wait_recv()
        y = 1 - yh
        part[g, 3, y] = add(part[g, 3, y], z2_v[g - 1, 0, y], z2_v[g - 1, 1, y]).astype(BF16)
        y_link.start(ys[g])

    def hand_over(g):
        outs[g].start()
        kept[g].start()

    def finish(g):
        ys[g].wait_recv()
        done_v[g] = add(part[g, 3, yh], z2_v[g - 1, 0, yh], z2_v[g - 1, 1, yh], y_v[g - 1]).astype(BF16)
        hand_over(g)

    def y_first(r):
        weight_grad(0, r)
        y_link.start(y0[r])

    def y_add(r):
        y0[r].wait_recv()
        part[0, r, yh] = add(part[0, r, yh], y0_v[r]).astype(BF16)

    def h_first():
        y_add(0)
        for i in range(2):
            z_links[i].start(h1[i])

    def h_raw():
        for i in range(2):
            y_add(1 + i)
            z_links[i].start(h2[i][1 - i])

    def h_second():
        for i in range(2):
            h1[i].wait_recv()
            part[0, 1 + i, yh, i] = add(part[0, 1 + i, yh, i], h1_v[i]).astype(BF16)
            z_links[i].start(h2[i][i])

    def h_finish():
        y_add(3)
        for i in range(2):
            for c in range(2):
                h2[i][c].wait_recv()
        done_v[0] = add(part[0, 3, yh], h2_v[0], h2_v[1]).astype(BF16)
        hand_over(0)

    def up_loop(refs, tile, first, last, count, use):
        def step(t, carry):
            @pl.when(t + 2 < count)
            def _():
                for copy in w_copies(refs, tile, t + 2):
                    copy.start()

            for copy in w_copies(refs, tile, t):
                copy.wait()
            use(t, lax.rem(t, 3))
            return carry

        lax.fori_loop(first, last, step, 0)

    def through(cots, slot, tile):
        return dot_last(cots[:, 0:512], w_v[slot, 0:tile, 0:512]) + dot_last(
            cots[:, HALF : HALF + 512], w_v[slot, 0:tile, 512:1024])

    def use_pre(t, slot):
        cols = pl.ds(pl.multiple_of(t * UP_TILE, UP_TILE), UP_TILE)
        up_v[:, :, cols] = through(grads, slot, UP_TILE).astype(BF16).reshape(SLOTS, ROWS, UP_TILE)

    def use_act(t, slot):
        cols = pl.ds(pl.multiple_of(t * ACT_TILE, ACT_TILE), ACT_TILE)
        aup_v[:, cols] = through(agrads, slot, ACT_TILE).astype(BF16)

    def act_loop():
        up_loop((aq, ak, av), ACT_TILE, 0, DA // ACT_TILE, DA // ACT_TILE, use_act)

    def pre_loop(half):
        count = D // UP_TILE
        up_loop((wq, wk, wv), UP_TILE, half * count // 2, (half + 1) * count // 2, count, use_pre)

    u1, u2, uy = [], [], []
    for p in range(2):
        cols = pl.ds(HALF_D * p, HALF_D)
        u1.append([
            remote(up_v.at[s, :, cols], u1_v.at[i, :, cols], u1_send.at[p, i], u1_recv.at[p, i], device)
            for i, (s, device) in enumerate(((4, x_right), (7, x_left)))])
        u2.append([
            remote(up_v.at[s, :, cols], u2_v.at[i, :, cols], u2_send.at[p, i], u2_recv.at[p, i], device)
            for i, (s, device) in enumerate(((3, x_right), (6, x_right), (2, x_left), (5, x_left)))])
        uy.append(remote(up_v.at[1, :, cols], uy_v.at[:, cols], uy_send.at[p], uy_recv.at[p], y_near))
    ay = remote(aup_v, ay_v, ay_send.at[0], ay_recv.at[0], y_near)
    ax = [
        remote(ax_v.at[0], ax_v.at[1 + i], ax_send.at[i], ax_recv.at[i], device)
        for i, device in enumerate((x_right, x_left, x_far))
    ]

    def up_step():
        ay.wait_recv()
        ax_v[0] = add(aup_v[...], ay_v[...]).astype(BF16)
        for copy in ax:
            copy.start()

    def up_start(p):
        pre_loop(p)
        for copy in (u1[p][0], u1[p][1], u2[p][1], u2[p][2]):
            copy.start()

    def up_add(p):
        cols = slice(HALF_D * p, HALF_D * (p + 1))
        for i, s in ((0, 3), (1, 5)):
            u1[p][i].wait_recv()
            up_v[s, :, cols] = add(up_v[s, :, cols], u1_v[i, :, cols]).astype(BF16)
        u2[p][0].start()
        u2[p][3].start()

    def up_last(p):
        cols = slice(HALF_D * p, HALF_D * (p + 1))
        for copy in u2[p]:
            copy.wait_recv()
        up_v[1, :, cols] = add(up_v[1, :, cols], u2_v[1, :, cols], u2_v[3, :, cols]).astype(BF16)
        uy[p].start()

    def before():
        act_loop()
        weight_grad(1, 0)

    greet((z_right, z_left, across, twin, x_right, x_left, x_far, y_near), before)
    z_first(1, compute=False)
    ay.start()
    prime((wq, wk, wv), UP_TILE)
    y_first(0)
    up_step()
    up_start(0)
    z_raw(1)
    up_start(1)
    for key in ((1, 0), (1, 1), (1, 2), (1, 3)):
        for copy in loads[key]:
            copy.start()
    y_first(1)
    z_first(2)
    z_second(1)
    y_first(2)
    up_add(0)
    y_first(3)
    up_add(1)
    z_raw(2)
    weight_grad(1, 3)
    y_last(1)
    weight_grad(2, 3)
    up_last(0)
    z_second(2)
    up_last(1)
    h_first()
    for copy in ax:
        copy.wait_recv()
    agrad[...] = norm_back(ain[...], again[...], add(ax_v[0], ax_v[3]) + add(ax_v[1], ax_v[2]))
    finish(1)
    h_raw()
    y_last(2)
    h_second()
    for copy in uy:
        copy.wait_recv()
    pgrad[...] = norm_back(pin[...], gain[...], add(up_v[0], u2_v[0], u2_v[2], uy_v[...]))
    finish(2)
    h_finish()

    for copy in (*u1[0], *u1[1], *u2[0], *u2[1], *uy, ay, *ax):
        copy.wait_send()
    for link in (*z_links, y_link):
        link.drain()
    for g in range(3):
        outs[g].wait()
        kept[g].wait()


def sum_everything(g_norm, g_cot, s_norm, s_cot, *rest):
    wide = tuple(m.reshape(PREF, D) for m in (g_norm, g_cot, s_norm, s_cot))
    dma = pltpu.SemaphoreType.DMA
    share = (2, SHARE, 256)
    row = (ROWS, D)

    def held(*shape):
        return pltpu.VMEM(shape, BF16)

    return pl.pallas_call(
        sum_kernel,
        out_shape=(
            jax.ShapeDtypeStruct(row, BF16), jax.ShapeDtypeStruct((ACT, DA), BF16),
            jax.ShapeDtypeStruct((2, 3, SHARE, 256), BF16),
        ),
        in_specs=[ANY] * 5 + [VMEM] * 11 + [ANY] * 6,
        out_specs=(VMEM, VMEM, ANY),
        scratch_shapes=[
            held(2, 4, 2 * PREF, Z_PRE), held(2, 2 * ACT, DA), held(2 * PREF, HALF), held(2 * ACT, HALF),
            held(3, ACT_TILE, 1024), held(3, 4, 2, *share), held(2, 2, *share), held(2, 2, 2, *share),
            held(*share), held(2, *share), held(4, *share), held(2, *share), held(3, *share), held(SLOTS, *row), held(2, *row), held(4, *row), held(*row),
            held(ACT, DA), held(ACT, DA), held(4, ACT, DA),
            dma((2, 4, 2)), dma((3, 6)), dma((1,)), dma((2, 2)), dma((2, 2)), dma((2, 2, 2)), dma((2, 2, 2)),
            dma((2,)), dma((2,)), dma((2, 2)), dma((2, 2)), dma((4,)), dma((4,)),
            dma((2,)), dma((2,)), dma((3,)), dma((3,)), dma((3,)),
            dma((2, 2)), dma((2, 2)), dma((2, 4)), dma((2, 4)), dma((2,)), dma((2,)),
            dma((1,)), dma((1,)), dma((3,)), dma((3,)),
        ],
        compiler_params=pltpu.CompilerParams(
            collective_id=1, has_side_effects=True, vmem_limit_bytes=62 << 20
        ),
        name="sum_everything",
    )(*wide, *rest)


def assemble_kernel(final, pgrad, agrad, *outs):
    outs[0][...] = pgrad[...]
    outs[1][...] = agrad[...]
    at = 2
    for rows in (slice(0, PRE), slice(PRE, SHARE)):
        for g, first, width in ((0, 0, 256), (1, 0, 128), (1, 128, 128), (2, 0, 256)):
            for h in range(2):
                outs[at][:, width * h : width * (h + 1)] = final[h, g, rows, first : first + width]
            at += 1


def assemble(final, pgrad, agrad):
    widths = (QW, KW, KW, QW)
    return pl.pallas_call(
        assemble_kernel,
        out_shape=tuple(
            [jax.ShapeDtypeStruct(pgrad.shape, BF16), jax.ShapeDtypeStruct(agrad.shape, BF16)]
            + [jax.ShapeDtypeStruct((rows, w), BF16) for rows in (PRE, ACTS) for w in widths]),
        in_specs=[VMEM] * 3,
        out_specs=(VMEM,) * 10,
        compiler_params=pltpu.CompilerParams(vmem_limit_bytes=32 << 20),
        name="assemble",
    )(final, pgrad, agrad)


def per_device(prefix_in, action_in, segment_ids, gain_prefix, gain_action, query_prefix, key_prefix, value_prefix,
               out_prefix, query_action, key_action, value_action, out_action, cot_prefix, cot_action):
    grads, agrads, s_grads, sa_grads, g_norm, g_cot, s_norm, s_cot, a_norm, sa_norm, sa_cot = gather_and_attend(
        prefix_in, cot_prefix, gain_prefix, action_in, cot_action, gain_action, segment_ids.reshape(SLOTS, ROWS),
        query_prefix, key_prefix, value_prefix, out_prefix, query_action, key_action, value_action, out_action)
    prefix_grad, action_grad, final = sum_everything(
        g_norm, g_cot, s_norm, s_cot, s_grads, a_norm, cot_action, sa_norm, sa_cot, grads, agrads, sa_grads,
        prefix_in, gain_prefix[None, :], action_in, gain_action[None, :],
        query_prefix, key_prefix, value_prefix, query_action, key_action, value_action)
    return assemble(final, prefix_grad, action_grad)


def solution(mesh):
    rows, sample, cols = P(("dp", "tensor"), None), P("dp", None), P(None, "tensor")
    in_specs = (rows, sample, sample, P(), P()) + (cols,) * 8 + (rows, sample)
    out_specs = (rows, sample) + (P("dp", "tensor"),) * 8
    return jax.shard_map(per_device, mesh=mesh, in_specs=in_specs, out_specs=out_specs, check_vma=False)
```

time: 216 us -> 182 us (0.84)
  Pallas kernels: 198 us -> 174 us
  local copies, waits for them, and re-layouts: 12.5 us -> 5.82 us
  other arithmetic: 4.34 us -> 1.34 us
    pallas_call x1, Pallas kernels: 114 us -> 91.9 us  [sum_everything(): pl.pallas_call(sum_kernel, out_shape=(jax.ShapeDtypeStruct(row, BF16), ja...]
    squeeze x4 -> x0, local copies, waits for them, and re-layouts: 3.99 us -> none  [both(): final[0, g, rows, cols]]
    concatenate x4 -> x0, other arithmetic: 2.98 us -> none  [both(): jnp.concatenate([final[0, g, rows, cols], final[1, g, rows, cols]], 1)]
    unnamed x15 -> x7, local copies, waits for them, and re-layouts: 6.15 us -> 3.8 us
where the time goes in v3:
time: 182 us
  Pallas kernels  174 us (96%)
  local copies, waits for them, and re-layouts  5.82 us (3%)
    pallas_call x1, Pallas kernels, sum_everything(): pl.pallas_call(sum_kernel, out_shape=(jax.ShapeDtypeStruct(row, BF16), ja...  91.9 us
    pallas_call x1, Pallas kernels, gather_and_attend(): pl.pallas_call(gather_kernel, out_shape=(jax.ShapeDtypeStruct((PREF, COLS...  80.3 us
    unnamed x7, local copies, waits for them, and re-layouts  3.8 us

profile of v3, /device:TPU:1, one launch (start us, length us, event | category | flops | bytes accessed | tf_op | source)
XLA Modules:
  0.0 181.6 jit_solution(10869576640800572884)
XLA Ops:
  0.6 0.5 broadcast.3
  1.2 1.3 reduce.3
  2.5 0.7 reshape.35.seg
  3.2 1.3 broadcast_in_dim.8.gain
  4.5 80.3 %gather_and_attend.1 = (bf16[512,1536]{1,0:T(8,128)(2,1)}, bf16[48,1536]{1,0:T(8,128)(2,1)}, bf16[512,768]{1,0:T(8,128)(2,1)}, bf16[48,768]{1,0:T(8,128)(2,1)}, ...) custom-call(bf16[64,4608]{1,0:T(8,128)(2,1)} %pin.3, ...), custom_call_target="tpu_custom_call" | custom-call | tf_op jit(solution)/shard_map/gather_and_attend/pallas_call | solution.py:309
  84.9 91.9 %sum_everything.1 = (bf16[64,4608]{1,0:T(8,128)(2,1)}, bf16[48,2048]{1,0:T(8,128)(2,1)}, bf16[2,3,416,256]{3,2,1,0:T(8,128)(2,1)}) custom-call(bf16[512,4608]{1,0:T(8,128)(2,1)} %bitcast.5, bf16[512,4608]{1,0:T(8,128)(2,1)} %bitcast.6, bf16[512,4608]{1,0:T(8,128)(2,1)} %bitcast.7, bf16[512,4608]{1,0:T(8,128)(2,1)} %bitcast.8, ...), custom_call_target="tpu_custom_call" | custom-call | tf_op jit(solution)/shard_map/sum_everything/pallas_call | solution.py:677
  176.8 0.0 copy-start
  176.8 1.3 copy-done
  178.1 0.0 copy-start.1
  178.1 1.1 copy-done.1
  179.2 0.0 copy-start.2
  179.2 0.9 copy-done.2
  180.1 1.5 assemble.1
Async XLA Ops:
  176.8 1.3 copy-start
  178.1 1.1 copy-start.1
  179.2 0.9 copy-start.2

commit v4 on v3

--- a/solution.py
+++ b/solution.py
@@ -154,7 +154,7 @@
 def gather_kernel(
     pin, cot, gain, ain, acot, again, seg, wq, wk, wv, wo, aq, ak, av, ao,
     grads, agrads, s_grads, sa_grads, g_norm, g_cot, s_norm, s_cot, a_norm, sa_norm, sa_cot,
-    norm_v, cot_v, w_v, aw_v, proj, aproj, dk, dv,
+    norm_v, cot_v, w_v, aw_v, proj, aproj, dk, dv, seg_v,
     send, recv, sib_send, sib_recv, local, w_sem, act_send, act_recv,
 ):
     weights = []
@@ -168,7 +168,7 @@
 
     def own_rows():
         cot_v[0] = cot[...]
-        norm_v[0] = norm(pin[...], gain[...])
+        norm_v[0] = norm(pin[...], gain[...].reshape(1, D))
 
     greet((left, right, across, twin), own_rows)
 
@@ -206,7 +206,7 @@
     spread(1, 0)
     spread(0, 0)
 
-    a_norm[...] = norm(ain[...], again[...])
+    a_norm[...] = norm(ain[...], again[...].reshape(1, DA))
     act_twins = [
         remote(a_norm, sa_norm, act_send.at[0], act_recv.at[0], twin),
         remote(acot, sa_cot, act_send.at[1], act_recv.at[1], twin),
@@ -279,8 +279,10 @@
         project(arrays[a][0], 4, 8, first)
 
     core = lax.rem(lax.axis_index("dp"), 2)
-    seg_row = jnp.concatenate([seg[pl.ds(s, 1), :] for s in slot_order()], 1).astype(F32)
-    seg_col = jnp.broadcast_to(seg_row, (8, PREF)).T[:, 0:1]
+    seg_v[...] = jnp.broadcast_to(seg[...].astype(F32), (HD, PREF)).T
+    seg_rows = jnp.concatenate(
+        [seg_v[pl.ds(pl.multiple_of(ROWS * s, ROWS), ROWS), :] for s in slot_order()], 0)
+    seg_col, seg_row = seg_rows[:, 0:1], seg_rows.T[0:1, :]
     attend(1 - core, proj, aproj, seg_row, seg_col, grads, agrads, dk, dv)
     theirs = pl.ds(pl.multiple_of((1 - core) * HALF, HALF), HALF)
     act_twins += [
@@ -319,7 +321,7 @@
             pltpu.VMEM((SLOTS, ROWS, D), BF16), pltpu.VMEM((SLOTS, ROWS, D), BF16),
             pltpu.VMEM((D, COLS), BF16), pltpu.VMEM((DA, COLS), BF16),
             pltpu.VMEM((SLOTS, ROWS, COLS), BF16), pltpu.VMEM((ACT, COLS), BF16),
-            pltpu.VMEM((PREF, HD), F32), pltpu.VMEM((PREF, HD), F32),
+            pltpu.VMEM((PREF, HD), F32), pltpu.VMEM((PREF, HD), F32), pltpu.VMEM((PREF, HD), F32),
             dma((2, SLOTS)), dma((2, SLOTS)), dma((2, SLOTS)), dma((2, SLOTS)), dma((2, SLOTS)),
             dma((8,)), dma((4,)), dma((4,)),
         ],
@@ -327,7 +329,7 @@
             collective_id=0, has_side_effects=True, vmem_limit_bytes=60 << 20
         ),
         name="gather_and_attend",
-    )(pin, cot, gain[None, :], ain, acot, again[None, :], seg, *weights)
+    )(pin, cot, gain, ain, acot, again, seg, *weights)
 
 
 SHARE = 416
@@ -373,7 +375,7 @@
     g_norm, g_cot, s_norm, s_cot, s_grads, a_norm, acot, sa_norm, sa_cot, grads, agrads, sa_grads, pin, gain, ain, again,
     wq, wk, wv, aq, ak, av,
     pgrad, agrad, final,
-    left_v, act_v, right_v, aright_v, w_v, part, z1_v, z2_v, h1_v, h2_v, y0_v, y_v, done_v, up_v, u1_v, u2_v, uy_v, aup_v, ay_v, ax_v,
+    left_v, act_v, right_v, aright_v, w_v, part, z1_v, z2_v, h1_v, h2_v, y0_v, y_v, done_v, up_v, u1_v, u2_v, uy_v, aup_v, ay_v, ax_v, gu_v, au_v,
     load_sem, w_sem, ex_sem, z1_send, z1_recv, z2_send, z2_recv, h1_send, h1_recv, h2_send, h2_recv, y0_send, y0_recv, y_send, y_recv, f_send, f_recv, f_local,
     u1_send, u1_recv, u2_send, u2_recv, uy_send, uy_recv, ay_send, ay_recv, ax_send, ax_recv,
 ):
@@ -395,12 +397,9 @@
         slot = lax.rem(t, 3)
         rows = pl.ds(pl.multiple_of(t * tile, tile), tile)
         copies = []
-        for h in range(2):
-            for j, (ref, width, first) in enumerate(zip(refs, (256, 128, 128), (0, 256, 384))):
-                copies.append(pltpu.make_async_copy(
-                    ref.at[rows, pl.ds(width * h, width)],
-                    w_v.at[slot, pl.ds(0, tile), pl.ds(512 * h + first, width)],
-                    w_sem.at[slot, 3 * h + j]))
+        for j, (ref, first) in enumerate(zip(refs, (0, QW, QW + KW))):
+            copies.append(pltpu.make_async_copy(
+                ref.at[rows], w_v.at[slot, pl.ds(0, tile), pl.ds(first, ref.shape[1])], w_sem.at[slot, j]))
         return copies
 
     def prime(refs, tile):
@@ -408,14 +407,16 @@
             for copy in w_copies(refs, tile, t):
                 copy.start()
 
-    prime((aq, ak, av), ACT_TILE)
     z_right, z_left, across, twin = z_step(1), z_step(-1), y_high(), sibling()
     x_right, x_left, x_far, y_near = x_step(1), x_step(-1), x_step(2), y_low()
     mine = pl.ds(pl.multiple_of(core * HALF, HALF), HALF)
     twin_half = pltpu.make_async_copy(s_grads, right_v.at[pl.ds(PREF, PREF)], ex_sem.at[0])
     twin_half.start()
-    for key in ((0, 0), (0, 1), (0, 2), (0, 3)):
-        for copy in loads[key]:
+    for copy in loads[0, 0]:
+        copy.start()
+    prime((aq, ak, av), ACT_TILE)
+    for r in range(1, 4):
+        for copy in loads[0, r]:
             copy.start()
     right_v[0:PREF] = grads[:, mine]
     aright_v[0:ACT] = agrads[:, mine]
@@ -530,7 +531,6 @@
             z_links[i].start(h2[i][i])
 
     def h_finish():
-        y_add(3)
         for i in range(2):
             for c in range(2):
                 h2[i][c].wait_recv()
@@ -551,17 +551,19 @@
 
         lax.fori_loop(first, last, step, 0)
 
-    def through(cots, slot, tile):
-        return dot_last(cots[:, 0:512], w_v[slot, 0:tile, 0:512]) + dot_last(
-            cots[:, HALF : HALF + 512], w_v[slot, 0:tile, 512:1024])
+    for h in range(2):
+        for first, width, to in ((0, 256, 256 * h), (256, 128, QW + 128 * h), (384, 128, QW + KW + 128 * h)):
+            cols = slice(HALF * h + first, HALF * h + first + width)
+            gu_v[:, to : to + width] = grads[:, cols]
+            au_v[:, to : to + width] = agrads[:, cols]
 
     def use_pre(t, slot):
         cols = pl.ds(pl.multiple_of(t * UP_TILE, UP_TILE), UP_TILE)
-        up_v[:, :, cols] = through(grads, slot, UP_TILE).astype(BF16).reshape(SLOTS, ROWS, UP_TILE)
+        up_v[:, :, cols] = dot_last(gu_v[...], w_v[slot, 0:UP_TILE]).astype(BF16).reshape(SLOTS, ROWS, UP_TILE)
 
     def use_act(t, slot):
         cols = pl.ds(pl.multiple_of(t * ACT_TILE, ACT_TILE), ACT_TILE)
-        aup_v[:, cols] = through(agrads, slot, ACT_TILE).astype(BF16)
+        aup_v[:, cols] = dot_last(au_v[...], w_v[slot, 0:ACT_TILE]).astype(BF16)
 
     def act_loop():
         up_loop((aq, ak, av), ACT_TILE, 0, DA // ACT_TILE, DA // ACT_TILE, use_act)
@@ -612,47 +614,45 @@
         up_v[1, :, cols] = add(up_v[1, :, cols], u2_v[1, :, cols], u2_v[3, :, cols]).astype(BF16)
         uy[p].start()
 
-    def before():
-        act_loop()
-        weight_grad(1, 0)
-
-    greet((z_right, z_left, across, twin, x_right, x_left, x_far, y_near), before)
+    greet((z_right, z_left, across, twin, x_right, x_left, x_far, y_near), lambda: weight_grad(1, 0))
     z_first(1, compute=False)
+    y_first(0)
+    act_loop()
     ay.start()
     prime((wq, wk, wv), UP_TILE)
-    y_first(0)
-    up_step()
     up_start(0)
     z_raw(1)
+    y_first(1)
     up_start(1)
     for key in ((1, 0), (1, 1), (1, 2), (1, 3)):
         for copy in loads[key]:
             copy.start()
-    y_first(1)
     z_first(2)
+    y_first(2)
     z_second(1)
-    y_first(2)
     up_add(0)
     y_first(3)
     up_add(1)
     z_raw(2)
     weight_grad(1, 3)
+    up_last(0)
     y_last(1)
     weight_grad(2, 3)
-    up_last(0)
+    up_last(1)
+    up_step()
     z_second(2)
-    up_last(1)
     h_first()
-    for copy in ax:
+    finish(1)
+    y_add(3)
+    for copy in uy:
         copy.wait_recv()
-    agrad[...] = norm_back(ain[...], again[...], add(ax_v[0], ax_v[3]) + add(ax_v[1], ax_v[2]))
-    finish(1)
+    pgrad[...] = norm_back(pin[...], gain[...].reshape(1, D), add(up_v[0], u2_v[0], u2_v[2], uy_v[...]))
     h_raw()
     y_last(2)
     h_second()
-    for copy in uy:
+    for copy in ax:
         copy.wait_recv()
-    pgrad[...] = norm_back(pin[...], gain[...], add(up_v[0], u2_v[0], u2_v[2], uy_v[...]))
+    agrad[...] = norm_back(ain[...], again[...].reshape(1, DA), add(ax_v[0], ax_v[3]) + add(ax_v[1], ax_v[2]))
     finish(2)
     h_finish()
 
@@ -686,8 +686,8 @@
             held(2, 4, 2 * PREF, Z_PRE), held(2, 2 * ACT, DA), held(2 * PREF, HALF), held(2 * ACT, HALF),
             held(3, ACT_TILE, 1024), held(3, 4, 2, *share), held(2, 2, *share), held(2, 2, 2, *share),
             held(*share), held(2, *share), held(4, *share), held(2, *share), held(3, *share), held(SLOTS, *row), held(2, *row), held(4, *row), held(*row),
-            held(ACT, DA), held(ACT, DA), held(4, ACT, DA),
-            dma((2, 4, 2)), dma((3, 6)), dma((1,)), dma((2, 2)), dma((2, 2)), dma((2, 2, 2)), dma((2, 2, 2)),
+            held(ACT, DA), held(ACT, DA), held(4, ACT, DA), held(PREF, 1024), held(ACT, 1024),
+            dma((2, 4, 2)), dma((3, 3)), dma((1,)), dma((2, 2)), dma((2, 2)), dma((2, 2, 2)), dma((2, 2, 2)),
             dma((2,)), dma((2,)), dma((2, 2)), dma((2, 2)), dma((4,)), dma((4,)),
             dma((2,)), dma((2,)), dma((3,)), dma((3,)), dma((3,)),
             dma((2, 2)), dma((2, 2)), dma((2, 4)), dma((2, 4)), dma((2,)), dma((2,)),
@@ -720,7 +720,7 @@
             + [jax.ShapeDtypeStruct((rows, w), BF16) for rows in (PRE, ACTS) for w in widths]),
         in_specs=[VMEM] * 3,
         out_specs=(VMEM,) * 10,
-        compiler_params=pltpu.CompilerParams(vmem_limit_bytes=32 << 20),
+        compiler_params=pltpu.CompilerParams(vmem_limit_bytes=60 << 20),
         name="assemble",
     )(final, pgrad, agrad)
 
@@ -728,11 +728,11 @@
 def per_device(prefix_in, action_in, segment_ids, gain_prefix, gain_action, query_prefix, key_prefix, value_prefix,
                out_prefix, query_action, key_action, value_action, out_action, cot_prefix, cot_action):
     grads, agrads, s_grads, sa_grads, g_norm, g_cot, s_norm, s_cot, a_norm, sa_norm, sa_cot = gather_and_attend(
-        prefix_in, cot_prefix, gain_prefix, action_in, cot_action, gain_action, segment_ids.reshape(SLOTS, ROWS),
+        prefix_in, cot_prefix, gain_prefix, action_in, cot_action, gain_action, segment_ids,
         query_prefix, key_prefix, value_prefix, out_prefix, query_action, key_action, value_action, out_action)
     prefix_grad, action_grad, final = sum_everything(
         g_norm, g_cot, s_norm, s_cot, s_grads, a_norm, cot_action, sa_norm, sa_cot, grads, agrads, sa_grads,
-        prefix_in, gain_prefix[None, :], action_in, gain_action[None, :],
+        prefix_in, gain_prefix, action_in, gain_action,
         query_prefix, key_prefix, value_prefix, query_action, key_action, value_action)
     return assemble(final, prefix_grad, action_grad)
 

time: 182 us -> 174 us (0.956)
  local copies, waits for them, and re-layouts: 5.82 us -> 0 us
    unnamed x7 -> x0, local copies, waits for them, and re-layouts: 3.8 us -> none
    pallas_call x1, Pallas kernels: 91.9 us -> 89.9 us  [sum_everything(): pl.pallas_call(sum_kernel, out_shape=(jax.ShapeDtypeStruct(row, BF16), ja...]
where the time goes in v4:
time: 174 us
  Pallas kernels  173 us (99%)
    pallas_call x1, Pallas kernels, sum_everything(): pl.pallas_call(sum_kernel, out_shape=(jax.ShapeDtypeStruct(row, BF16), ja...  89.9 us
    pallas_call x1, Pallas kernels, gather_and_attend(): pl.pallas_call(gather_kernel, out_shape=(jax.ShapeDtypeStruct((PREF, COLS...  80.4 us

profile of v4, /device:TPU:1, one launch (start us, length us, event | category | flops | bytes accessed | tf_op | source)
XLA Modules:
  0.0 173.8 jit_solution(11348783192491191935)
XLA Ops:
  0.6 80.4 %gather_and_attend.1 = (bf16[512,1536]{1,0:T(8,128)(2,1)}, bf16[48,1536]{1,0:T(8,128)(2,1)}, bf16[512,768]{1,0:T(8,128)(2,1)}, bf16[48,768]{1,0:T(8,128)(2,1)}, ...) custom-call(bf16[64,4608]{1,0:T(8,128)(2,1)} %pin.3, ...), custom_call_target="tpu_custom_call" | custom-call | tf_op jit(solution)/shard_map/gather_and_attend/pallas_call | solution.py:311
  81.1 89.9 %sum_everything.1 = (bf16[64,4608]{1,0:T(8,128)(2,1)}, bf16[48,2048]{1,0:T(8,128)(2,1)}, bf16[2,3,416,256]{3,2,1,0:T(8,128)(2,1)}) custom-call(bf16[512,4608]{1,0:T(8,128)(2,1)} %bitcast.4, bf16[512,4608]{1,0:T(8,128)(2,1)} %bitcast.5, bf16[512,4608]{1,0:T(8,128)(2,1)} %bitcast.6, bf16[512,4608]{1,0:T(8,128)(2,1)} %bitcast.7, ...), custom_call_target="tpu_custom_call" | custom-call | tf_op jit(solution)/shard_map/sum_everything/pallas_call | solution.py:677
  171.0 2.8 %assemble.1 = (bf16[64,4608]{1,0:T(8,128)(2,1)}, bf16[48,2048]{1,0:T(8,128)(2,1)}, bf16[288,512]{1,0:T(8,128)(2,1)}, bf16[288,256]{1,0:T(8,128)(2,1)}, bf16[288,...) custom-call(bf16[2,3,416,256]{3,2,1,0:T(8,128)(2,1)} %get-tuple-elem, ...), custom_call_target="tpu_custom_call" | custom-call | tf_op jit(solution)/shard_map/assemble/pallas_call | solution.py:716

commit v5 on v4

--- a/solution.py
+++ b/solution.py
@@ -91,12 +91,30 @@
     return t, jnp.exp(SOFT_CAP * t)
 
 
-def attend(h, proj, aproj, seg_row, seg_col, grads, agrads, dk, dv):
-    block = 256
-
-    def cols(first, width=HD):
-        return pl.ds(pl.multiple_of(first, HD), width)
-
+BLOCK = 256
+
+
+def cols(first, width=HD):
+    return pl.ds(pl.multiple_of(first, HD), width)
+
+
+def attend_forward(i, h, proj, seg_row, seg_col, grads, probs, tanhs):
+    key = proj[:, :, cols(QW + HD * h)].reshape(PREF, HD)
+    value_t = proj[:, :, cols(QW + KW + HD * h)].reshape(PREF, HD).T
+    for g in range(2):
+        for b in range(PREF // BLOCK):
+            rows = slice(b * BLOCK, (b + 1) * BLOCK)
+            slots = slice(b * BLOCK // ROWS, (b + 1) * BLOCK // ROWS)
+            t, w = soft(key, proj[slots, :, cols(HD * (2 * h + g))].reshape(BLOCK, HD))
+            w = jnp.where(seg_col <= seg_row[:, rows], w, 0.0)
+            p = w * (1.0 / jnp.sum(w, 0, keepdims=True))
+            tanhs[i, g, :, rows] = t
+            probs[i, g, :, rows] = p
+            at = jnp.dot(value_t, p.astype(BF16), preferred_element_type=F32).T
+            grads[rows, cols(HALF * h + 512 + HD * g)] = at.astype(BF16)
+
+
+def attend(i, h, proj, aproj, probs, tanhs, grads, agrads, dk, dv):
     key = proj[:, :, cols(QW + HD * h)].reshape(PREF, HD)
     value = proj[:, :, cols(QW + KW + HD * h)].reshape(PREF, HD)
     key_t, value_t = key.T, value.T
@@ -128,25 +146,20 @@
         agrads[:, cols(base + 512 + HD * g)] = aat[ACT * g : ACT * (g + 1)].astype(BF16)
 
     for g in range(2):
-        for b in range(PREF // block):
-            rows = slice(b * block, (b + 1) * block)
-            slots = slice(b * block // ROWS, (b + 1) * block // ROWS)
+        for b in range(PREF // BLOCK):
+            rows = slice(b * BLOCK, (b + 1) * BLOCK)
+            slots = slice(b * BLOCK // ROWS, (b + 1) * BLOCK // ROWS)
             first = HD * (2 * h + g)
-            query = proj[slots, :, cols(first)].reshape(block, HD)
-            dout = proj[slots, :, cols(QW + 2 * KW + first)].reshape(block, HD)
-            t, w = soft(key, query)
-            w = jnp.where(seg_col <= seg_row[:, rows], w, 0.0)
-            p = w * (1.0 / jnp.sum(w, 0, keepdims=True))
+            query = proj[slots, :, cols(first)].reshape(BLOCK, HD)
+            dout = proj[slots, :, cols(QW + 2 * KW + first)].reshape(BLOCK, HD)
+            t, p = tanhs[i, g, :, rows], probs[i, g, :, rows]
             gp = dot_last(value, dout)
             inner = jnp.sum(p * gp, 0, keepdims=True)
             s = (p * (gp - inner) * (1.0 - t * t) * SCALE).astype(BF16)
-            p = p.astype(BF16)
             dk[...] += jnp.dot(s, query, preferred_element_type=F32)
-            dv[...] += jnp.dot(p, dout, preferred_element_type=F32)
+            dv[...] += jnp.dot(p.astype(BF16), dout, preferred_element_type=F32)
             dq = jnp.dot(key_t, s, preferred_element_type=F32).T
-            at = jnp.dot(value_t, p, preferred_element_type=F32).T
             grads[rows, cols(base + HD * g)] = dq.astype(BF16)
-            grads[rows, cols(base + 512 + HD * g)] = at.astype(BF16)
     grads[:, cols(base + 256)] = dk[...].astype(BF16)
     grads[:, cols(base + 384)] = dv[...].astype(BF16)
 
@@ -154,7 +167,7 @@
 def gather_kernel(
     pin, cot, gain, ain, acot, again, seg, wq, wk, wv, wo, aq, ak, av, ao,
     grads, agrads, s_grads, sa_grads, g_norm, g_cot, s_norm, s_cot, a_norm, sa_norm, sa_cot,
-    norm_v, cot_v, w_v, aw_v, proj, aproj, dk, dv, seg_v,
+    norm_v, cot_v, w_v, aw_v, proj, aproj, dk, dv, seg_v, probs, tanhs,
     send, recv, sib_send, sib_recv, local, w_sem, act_send, act_recv,
 ):
     weights = []
@@ -256,6 +269,8 @@
     hops[0][5].start()
     hops[1][4].wait_send()
     hops[0][6].start()
+    hops[1][5].start()
+    hops[1][6].start()
     for a in range(2):
         hops[a][4].wait_recv()
         hops[a][7].start()
@@ -267,23 +282,24 @@
     spread(1, 2)
     spread(0, 3)
     project(norm_v, 0, 4, 0)
-    hops[0][5].wait_send()
-    hops[1][5].start()
-    hops[0][6].wait_send()
-    hops[1][6].start()
     project(cot_v, 0, 4, 4)
+    for s in (5, 6):
+        hops[0][s].wait_send()
+    core = lax.rem(lax.axis_index("dp"), 2)
+    seg_v[...] = jnp.broadcast_to(seg[...].astype(F32), (HD, PREF)).T
+    seg_rows = jnp.concatenate(
+        [seg_v[pl.ds(pl.multiple_of(ROWS * s, ROWS), ROWS), :] for s in slot_order()], 0)
+    seg_col, seg_row = seg_rows[:, 0:1], seg_rows.T[0:1, :]
     for a, first in ((0, 0), (1, 4)):
         for s in (5, 6, 7):
             hops[a][s].wait_recv()
             spread(a, s)
         project(arrays[a][0], 4, 8, first)
-
-    core = lax.rem(lax.axis_index("dp"), 2)
-    seg_v[...] = jnp.broadcast_to(seg[...].astype(F32), (HD, PREF)).T
-    seg_rows = jnp.concatenate(
-        [seg_v[pl.ds(pl.multiple_of(ROWS * s, ROWS), ROWS), :] for s in slot_order()], 0)
-    seg_col, seg_row = seg_rows[:, 0:1], seg_rows.T[0:1, :]
-    attend(1 - core, proj, aproj, seg_row, seg_col, grads, agrads, dk, dv)
+        if a == 0:
+            for i, h in enumerate((1 - core, core)):
+                attend_forward(i, h, proj, seg_row, seg_col, grads, probs, tanhs)
+
+    attend(0, 1 - core, proj, aproj, probs, tanhs, grads, agrads, dk, dv)
     theirs = pl.ds(pl.multiple_of((1 - core) * HALF, HALF), HALF)
     act_twins += [
         remote(grads.at[:, theirs], s_grads, act_send.at[2], act_recv.at[2], twin),
@@ -291,7 +307,7 @@
     ]
     for copy in act_twins[2:]:
         copy.start()
-    attend(core, proj, aproj, seg_row, seg_col, grads, agrads, dk, dv)
+    attend(1, core, proj, aproj, probs, tanhs, grads, agrads, dk, dv)
     for a in range(2):
         hops[a][1].wait_send()
         hops[a][7].wait_send()
@@ -322,6 +338,7 @@
             pltpu.VMEM((D, COLS), BF16), pltpu.VMEM((DA, COLS), BF16),
             pltpu.VMEM((SLOTS, ROWS, COLS), BF16), pltpu.VMEM((ACT, COLS), BF16),
             pltpu.VMEM((PREF, HD), F32), pltpu.VMEM((PREF, HD), F32), pltpu.VMEM((PREF, HD), F32),
+            pltpu.VMEM((2, 2, PREF, PREF), F32), pltpu.VMEM((2, 2, PREF, PREF), F32),
             dma((2, SLOTS)), dma((2, SLOTS)), dma((2, SLOTS)), dma((2, SLOTS)), dma((2, SLOTS)),
             dma((8,)), dma((4,)), dma((4,)),
         ],

time: 174 us -> 174 us (level)
  no operation moved by 1% of the time
where the time goes in v5:
time: 174 us; the launch traced here: 173 us
  Pallas kernels  173 us (99%)
    pallas_call x1, Pallas kernels, sum_everything(): pl.pallas_call(sum_kernel, out_shape=(jax.ShapeDtypeStruct(row, BF16), ja...  89.9 us
    pallas_call x1, Pallas kernels, gather_and_attend(): pl.pallas_call(gather_kernel, out_shape=(jax.ShapeDtypeStruct((PREF, COLS...  80.1 us

profile of v5, /device:TPU:1, one launch (start us, length us, event | category | flops | bytes accessed | tf_op | source)
XLA Modules:
  0.0 173.5 jit_solution(16014868834214395256)
XLA Ops:
  0.6 80.1 %gather_and_attend.1 = (bf16[512,1536]{1,0:T(8,128)(2,1)}, bf16[48,1536]{1,0:T(8,128)(2,1)}, bf16[512,768]{1,0:T(8,128)(2,1)}, bf16[48,768]{1,0:T(8,128)(2,1)}, ...) custom-call(bf16[64,4608]{1,0:T(8,128)(2,1)} %pin.3, ...), custom_call_target="tpu_custom_call" | custom-call | tf_op jit(solution)/shard_map/gather_and_attend/pallas_call | solution.py:327
  80.7 89.9 %sum_everything.1 = (bf16[64,4608]{1,0:T(8,128)(2,1)}, bf16[48,2048]{1,0:T(8,128)(2,1)}, bf16[2,3,416,256]{3,2,1,0:T(8,128)(2,1)}) custom-call(bf16[512,4608]{1,0:T(8,128)(2,1)} %bitcast.4, bf16[512,4608]{1,0:T(8,128)(2,1)} %bitcast.5, bf16[512,4608]{1,0:T(8,128)(2,1)} %bitcast.6, bf16[512,4608]{1,0:T(8,128)(2,1)} %bitcast.7, ...), custom_call_target="tpu_custom_call" | custom-call | tf_op jit(solution)/shard_map/sum_everything/pallas_call | solution.py:694
  170.6 2.8 %assemble.1 = (bf16[64,4608]{1,0:T(8,128)(2,1)}, bf16[48,2048]{1,0:T(8,128)(2,1)}, bf16[288,512]{1,0:T(8,128)(2,1)}, bf16[288,256]{1,0:T(8,128)(2,1)}, bf16[288,...) custom-call(bf16[2,3,416,256]{3,2,1,0:T(8,128)(2,1)} %get-tuple-elem, ...), custom_call_target="tpu_custom_call" | custom-call | tf_op jit(solution)/shard_map/assemble/pallas_call | solution.py:733
